TPU v7x, 512 devices: a whole 4x4x16 slice. The times are simulated.
512 devices in a mesh: img: 16 (over z), unit: 32 (over y, x, core).
Axes of the slice: x: 4, y: 4, z: 16, core: 2. Of those that a mesh axis runs over, the one named last changes fastest.
Arguments:
- tokens: bfloat16 [16, 768, 16, 288], P('img', 'unit'), may hold values from -6 to 6
- live: int32 [16, 32], P('img', 'unit'), may hold values from 0 to 24, as said below
- cotangent: bfloat16 [16, 384, 4, 576], P('img', 'unit'), may hold values from -6 to 6
- w_qkv: bfloat16 [288, 864], replicated, may hold values from -0.375 to 0.375
- w_out: bfloat16 [288, 288], replicated, may hold values from -0.375 to 0.375
- w_pool: bfloat16 [288, 576], replicated, may hold values from -0.375 to 0.375
- gain_one: float32 [288], replicated, may hold values from 0.1 to 1.9
- gain_two: float32 [288], replicated, may hold values from 0.1 to 1.9
Outputs:
- pooled: bfloat16 [16, 384, 4, 576], P('img', 'unit')
- grad_tokens: bfloat16 [16, 768, 16, 288], P('img', 'unit')
- grad_qkv: float32 [288, 864], replicated
- grad_out: float32 [288, 288], replicated
- grad_pool: float32 [288, 576], replicated
- grad_gain_one: float32 [288], replicated
- grad_gain_two: float32 [288], replicated
Inputs may be any that keep to these rules, and one draw needn't show every extreme that they name: The counts of an image sum to 384; for every unit shard j, the kept units before it, start = live[i, 0] + ... + live[i, j-1], number between j * 12 and (j + 1) * 12.
All inputs are finite; a program needn't handle non-finite values.
Results may differ from a plain program's by a relative error of at most 0.009.
Values may be sent and summed in bfloat16 or wider, within the bound.
A program may use at most 64 MiB of HBM per device.

v0:
```python
import math

import jax
import jax.numpy as jnp
from jax import lax
from jax.sharding import PartitionSpec as P

HEADS = 4
HEAD_DIM = 72


EPSILON = 1e-06


def prefix(shard, axis, combine, identity):
    peers, position = (lax.axis_size(axis), lax.axis_index(axis))
    everything = lax.all_gather(shard, axis)
    start = jnp.broadcast_to(jnp.asarray(identity, shard.dtype), shard.shape)

    def turn(k, before):
        reached = k < position
        new = combine(before, everything[k])
        return jnp.where(reached, new, before)

    return lax.fori_loop(0, peers, turn, start)


def from_behind(block, axis, distance):
    devices = range(lax.axis_size(axis))
    route = [(i - distance, i) for i in devices if i - distance in devices]
    return lax.ppermute(block, axis, route)


def normalize(values):
    average = jnp.mean(values, axis=-1, keepdims=True)
    centred = values - average
    inv_scale = lax.rsqrt(jnp.mean(centred * centred, axis=-1, keepdims=True) + EPSILON)
    return (centred * inv_scale, inv_scale)


def norm_back(grad_norm, normed_v, inv_scale):
    first = jnp.mean(grad_norm, axis=-1, keepdims=True)
    second = jnp.mean(grad_norm * normed_v, axis=-1, keepdims=True)
    return inv_scale * (grad_norm - first - normed_v * second)


def pool_grid(values):
    unit_count, width = (values.shape[0], values.shape[-1])
    return jnp.mean(values.reshape(unit_count, 2, 2, 2, 2, width), axis=(2, 4)).reshape(
        unit_count, 4, width
    )


def spread_grid(values):
    unit_count, width = (values.shape[0], values.shape[-1])
    grid = jnp.broadcast_to(
        values.reshape(unit_count, 2, 1, 2, 1, width), (unit_count, 2, 2, 2, 2, width)
    )
    return grid.reshape(unit_count, 16, width) * 0.25


def mult(form, left, right):
    return jnp.einsum(form, left, right, preferred_element_type=jnp.float32)


def forward(unit_rows, w_qkv, w_out, w_pool, gain_one, gain_two):
    unit_count, token_count, width = unit_rows.shape
    tokens_f = unit_rows.astype(jnp.float32)
    norm_one, scale_one = normalize(tokens_f)
    normed = (norm_one * gain_one).astype(jnp.bfloat16)
    proj_qkv = jnp.dot(normed.reshape(-1, width), w_qkv, preferred_element_type=jnp.float32).astype(
        jnp.bfloat16
    )
    proj_qkv = proj_qkv.reshape(unit_count, token_count, 3, HEADS, HEAD_DIM)
    query_part, key_part, value_part = (proj_qkv[:, :, 0], proj_qkv[:, :, 1], proj_qkv[:, :, 2])
    factor = HEAD_DIM ** (-0.5)
    scores = mult("uthd,ushd->uhts", query_part, key_part) * factor
    attend = jax.nn.softmax(scores, axis=-1)
    attend_b = attend.astype(jnp.bfloat16)
    mixed_heads = (
        mult("uhts,ushd->uthd", attend_b, value_part)
        .astype(jnp.bfloat16)
        .reshape(unit_count, token_count, width)
    )
    residual = tokens_f + jnp.dot(
        mixed_heads.reshape(-1, width), w_out, preferred_element_type=jnp.float32
    ).reshape(unit_count, token_count, width)
    norm_two, scale_two = normalize(residual)
    grouped = pool_grid(norm_two * gain_two).astype(jnp.bfloat16)
    pooled = jnp.dot(grouped.reshape(-1, width), w_pool, preferred_element_type=jnp.float32).astype(
        jnp.bfloat16
    )
    pooled = pooled.reshape(unit_count, 4, w_pool.shape[1])
    saved = (
        norm_one,
        scale_one,
        normed,
        query_part,
        key_part,
        value_part,
        attend,
        attend_b,
        mixed_heads,
        norm_two,
        scale_two,
        grouped,
    )
    return (pooled, saved)


def backward(saved, cotangent, w_qkv, w_out, w_pool, gain_one, gain_two):
    (
        norm_one,
        scale_one,
        normed,
        query_part,
        key_part,
        value_part,
        attend,
        attend_b,
        mixed_heads,
        norm_two,
        scale_two,
        grouped,
    ) = saved
    unit_count, token_count, width = norm_one.shape
    out_width = w_pool.shape[1]
    factor = HEAD_DIM ** (-0.5)
    cot_rows = cotangent.reshape(-1, out_width)
    grad_pool = jnp.dot(grouped.reshape(-1, width).T, cot_rows, preferred_element_type=jnp.float32)
    grad_grouped = jnp.dot(cot_rows, w_pool.T, preferred_element_type=jnp.float32).reshape(
        unit_count, 4, width
    )
    grad_scaled = spread_grid(grad_grouped)
    grad_gain_two = jnp.sum(grad_scaled * norm_two, axis=(0, 1))
    grad_resid = norm_back(grad_scaled * gain_two, norm_two, scale_two)
    resid_b = grad_resid.astype(jnp.bfloat16).reshape(-1, width)
    grad_out = jnp.dot(
        mixed_heads.reshape(-1, width).T, resid_b, preferred_element_type=jnp.float32
    )
    grad_mixed = jnp.dot(resid_b, w_out.T, preferred_element_type=jnp.float32).astype(jnp.bfloat16)
    grad_mixed = grad_mixed.reshape(unit_count, token_count, HEADS, HEAD_DIM)
    grad_attend = mult("uthd,ushd->uhts", grad_mixed, value_part)
    grad_value = mult("uhts,uthd->ushd", attend_b, grad_mixed).astype(jnp.bfloat16)
    grad_scores = (
        attend * (grad_attend - jnp.sum(grad_attend * attend, axis=-1, keepdims=True)) * factor
    ).astype(jnp.bfloat16)
    grad_query = mult("uhts,ushd->uthd", grad_scores, key_part).astype(jnp.bfloat16)
    grad_key = mult("uhts,uthd->ushd", grad_scores, query_part).astype(jnp.bfloat16)
    grad_proj = jnp.stack([grad_query, grad_key, grad_value], axis=2).reshape(-1, 3 * width)
    grad_qkv = jnp.dot(normed.reshape(-1, width).T, grad_proj, preferred_element_type=jnp.float32)
    grad_normed = jnp.dot(grad_proj, w_qkv.T, preferred_element_type=jnp.float32).reshape(
        unit_count, token_count, width
    )
    grad_gain_one = jnp.sum(grad_normed * norm_one, axis=(0, 1))
    grad_input = norm_back(grad_normed * gain_one, norm_one, scale_one)
    grad_tokens = (grad_resid + grad_input).astype(jnp.bfloat16)
    return (grad_tokens, (grad_qkv, grad_out, grad_pool, grad_gain_one, grad_gain_two))


def add_counts(earlier, later):
    return earlier + later


def pick_forward(offsets, counts, first_rank, out_slots, slots):
    rank_ids = first_rank + jnp.arange(out_slots, dtype=jnp.int32)
    position = rank_ids[None, :] - offsets
    usable = (position >= 0) & (position < counts)
    columns = jnp.arange(slots, dtype=jnp.int32)
    hits = usable[:, :, None] & (position[:, :, None] == columns[None, None, :])
    return hits.astype(jnp.bfloat16)


def pick_backward(offsets, counts, first_rank, out_slots, slots):
    slot_ids = jnp.arange(slots, dtype=jnp.int32)
    position = offsets + slot_ids[None, :] - first_rank
    usable = (slot_ids[None, :] < counts) & (position >= 0) & (position < out_slots)
    columns = jnp.arange(out_slots, dtype=jnp.int32)
    hits = usable[:, :, None] & (position[:, :, None] == columns[None, None, :])
    return hits.astype(jnp.bfloat16)


def move_rows(select, data):
    flat = data.reshape(data.shape[0], data.shape[1], -1)
    moved = jnp.einsum("ibs,isf->ibf", select, flat, preferred_element_type=jnp.float32)
    return moved.astype(jnp.bfloat16).reshape(select.shape[:2] + data.shape[2:])


def last_rows(data, offsets, live, keep):
    begin = jnp.clip(live - keep, 0, data.shape[1] - keep)
    rows = jax.vmap(lambda block, first: block)(data, begin[:, 0])
    return (rows, offsets + begin, live - begin)


def local(tokens, live, cotangent, w_qkv, w_out, w_pool, gain_one, gain_two):
    img_dev, slots, token_count, width = tokens.shape
    out_slots = cotangent.shape[1]
    base_rank = lax.axis_index("unit") * out_slots
    offsets = prefix(live, "unit", add_counts, jnp.zeros_like(live))
    take_own = pick_forward(offsets, live, base_rank, out_slots, slots)
    back_own = pick_backward(offsets, live, base_rank, out_slots, slots)
    back_next = pick_backward(offsets, live, base_rank + out_slots, out_slots, slots)
    pooled_slots, saved = forward(
        tokens.reshape(-1, token_count, width), w_qkv, w_out, w_pool, gain_one, gain_two
    )
    pooled_slots = pooled_slots.reshape(img_dev, slots, 4, cotangent.shape[3])
    sent_rows, sent_offsets, sent_live = last_rows(pooled_slots, offsets, live, slots)
    prev_pooled, prev_offsets, prev_live = from_behind(
        (sent_rows, sent_offsets, sent_live), "unit", 1
    )
    take_prev = pick_forward(prev_offsets, prev_live, base_rank, out_slots, slots)
    pooled = move_rows(take_own, pooled_slots) + move_rows(take_prev, prev_pooled)
    next_cot = from_behind(cotangent, "unit", -1)
    cot_slots = move_rows(back_own, cotangent) + move_rows(back_next, next_cot)
    grad_units, grads = backward(
        saved,
        cot_slots.reshape(-1, 4, cotangent.shape[3]),
        w_qkv,
        w_out,
        w_pool,
        gain_one,
        gain_two,
    )
    grad_tokens = grad_units.reshape(tokens.shape)
    totals = lax.psum((grads[0], grads[1], grads[2], grads[3], grads[4]), ("img", "unit"))
    factor = 1.0 / math.sqrt(img_dev * lax.axis_size("img") * out_slots * lax.axis_size("unit"))
    return (
        pooled,
        grad_tokens,
        totals[0] * factor,
        totals[1] * factor,
        totals[2] * factor,
        totals[3] * factor,
        totals[4] * factor,
    )


def solution(mesh):
    return jax.shard_map(
        local,
        mesh=mesh,
        in_specs=(
            P("img", "unit", None, None),
            P("img", "unit"),
            P("img", "unit", None, None),
            P(),
            P(),
            P(),
            P(),
            P(),
        ),
        out_specs=(
            P("img", "unit", None, None),
            P("img", "unit", None, None),
            P(),
            P(),
            P(),
            P(),
            P(),
        ),
        check_vma=False,
    )
```

profile of v0, /device:TPU:1, one launch (start us, length us, event | category | flops | bytes accessed | tf_op | source)
XLA Modules:
  0.0 610.8 jit_solution(3345122187023899411)
XLA Ops:
  7.3 8.9 %collective-permute-start.3 = (bf16[1,12,4,576]{3,2,1,0:T(4,128)(2,1)}, bf16[1,12,4,576]{3,2,1,0:T(4,128)(2,1)S(1)}, u32[]{:S(2)}, u32[]{:S(2)}) collective-permute-start(bf16[1,12,4,576]{3,2,1,0:T(4,128)(2,1)} %param.12), channel_id=1, source_target_pairs={{1,0},{2,1},{3,2},{4,3},{5,4},{6,5},{7,6},{8,7},{9,8},{10,9},{11,1... | collective-permute-start | bytes 165896 | tf_op jit(solution)/shard_map/ppermute | solution.py:31
  16.8 1.3 dynamic-slice
  18.8 8.1 %all-reduce = s32[32]{0:T(128)S(1)} all-reduce(s32[32]{0:T(128)S(1)} %bitcast_dynamic-update-slice_fusion), channel_id=2, replica_groups=mesh['img'=16,'unit'=32] {'unit'}, use_global_device_ids=true, to_apply=%add | all-reduce | flops 32 | bytes 256
  26.9 40.2 %while.13 = (s32[]{:T(128)}, s32[1,1]{1,0:T(1,128)}, s32[]{:T(128)}, s32[32,1,1]{0,2,1:T(1,128)S(1)}, s32[]{:T(128)}) while((s32[]{:T(128)}, s32[1,1]{1,0:T(1,128)}, s32[]{:T(128)}, s32[32,1,1]{0,2,1:T(1,128)S(1)}, s32[]{:T(128)}) %tuple.57), condition=%wide.region_1.2_spmd, body=%wide.region_0.1_spmd.sunk | while | flops 5 | bytes 107 | solution.py:25
  67.1 6.2 %collective-permute-start = (s32[1,1]{1,0:T(1,128)}, s32[1,1]{1,0:T(1,128)}, u32[]{:S(2)}, u32[]{:S(2)}) collective-permute-start(s32[1,1]{1,0:T(1,128)} %add.155), channel_id=1, source_target_pairs={{0,1},{1,2},{2,3},{3,4},{4,5},{5,6},{6,7},{7,8},{8,9},{9,10},{10,1... | collective-permute-start | bytes 20 | tf_op jit(solution)/shard_map/ppermute | solution.py:31
  73.3 2.7 collective-permute-start.1
  76.0 1.1 convert_reduce_fusion
  77.1 1.2 fusion.33
  78.4 0.9 reshape.601
  79.4 1.6 fusion.36
  82.2 1.1 reshape.597
  88.3 1.0 reshape_reshape.10
  92.8 0.9 copy.71
  93.7 1.2 reshape.606
  95.0 1.2 fusion.44
  96.2 3.3 fusion.11
  99.5 2.7 fusion.12
  102.2 2.2 fusion.13
  105.2 1.4 pad_maximum_fusion
  107.2 1.6 dot_general.77
  108.8 1.5 reshape.608
  110.3 2.4 fusion.32
  112.7 1.4 fusion.47
  115.2 1.1 fusion.91
  116.3 1.1 fusion.92
  117.5 1.4 fusion.90
  119.0 1.4 compare_and_fusion.2
  120.8 4.0 collective-permute-start.2
  124.8 107.9 %all-reduce.1 = (f32[288]{0:T(512)S(1)}, f32[288]{0:T(512)S(1)}) all-reduce(f32[288]{0:T(512)S(1)} %copy-done.22, f32[288]{0:T(512)S(1)} %get-tuple-element.103), channel_id=1, replica_groups=mesh['img'=16,'unit'=32] {'img','unit'}, use_global_device_ids=true, to_apply=%region_18.19 | all-reduce | flops 576 | bytes 4608 | tf_op jit(solution)/shard_map/psum | solution.py:225
  234.7 365.0 %all-reduce.5.cloned.1.call-done = (f32[288,864]{1,0:T(8,128)}, f32[288,288]{1,0:T(8,128)}, f32[288,576]{1,0:T(8,128)}) async-done(((f32[288,864]{1,0:T(8,128)}, f32[288,288]{1,0:T(8,128)}, f32[288,576]{1,0:T(8,128)}), (f32[288,864]{1,0:T(8,128)}, f32[288,288]{1,0:T(8,128)}, f32[288,576]{1,0:T(8,128)})) %all-reduce.5.cloned.1.call-update) | async-done | bytes 1990672 | tf_op jit(solution)/shard_map/psum | solution.py:225
  599.7 2.3 broadcast_multiply_fusion
  602.0 0.9 broadcast_multiply_fusion.1
  (142 shorter events, 34.9 us)
Async XLA Ops:
  7.2 74.0 %copy-start = (bf16[288,864]{1,0:T(8,128)(2,1)S(1)}, bf16[288,864]{1,0:T(8,128)(2,1)}, u32[]{:S(2)}) copy-start(bf16[288,864]{1,0:T(8,128)(2,1)} %param.13) | copy-start | bytes 1492996
  7.2 72.3 %copy-start.1 = (bf16[1,24,16,288]{3,2,1,0:T(8,128)(2,1)S(1)}, bf16[1,24,16,288]{3,2,1,0:T(8,128)(2,1)}, u32[]{:S(2)}) copy-start(bf16[1,24,16,288]{3,2,1,0:T(8,128)(2,1)} %param.10) | copy-start | bytes 663556
  7.2 73.8 %copy-start.18 = (f32[288]{0:T(512)S(1)}, f32[288]{0:T(512)}, u32[]{:S(2)}) copy-start(f32[288]{0:T(512)} %param.16) | copy-start | bytes 3460
  7.2 592.5 %all-reduce.5.cloned.1.call-start = ((), (), s32[]{:S(2)}) async-start(), calls=%async_computation | async-start | bytes 4423680 | tf_op jit(solution)/shard_map/psum | solution.py:225
  7.3 82.0 %collective-permute-start.3 = (bf16[1,12,4,576]{3,2,1,0:T(4,128)(2,1)}, bf16[1,12,4,576]{3,2,1,0:T(4,128)(2,1)S(1)}, u32[]{:S(2)}, u32[]{:S(2)}) collective-permute-start(bf16[1,12,4,576]{3,2,1,0:T(4,128)(2,1)} %param.12), channel_id=1, source_target_pairs={{1,0},{2,1},{3,2},{4,3},{5,4},{6,5},{7,6},{8,7},{9,8},{10,9},{11,1... | collective-permute-start | bytes 165896 | tf_op jit(solution)/shard_map/ppermute | solution.py:31
  67.1 51.9 %collective-permute-start = (s32[1,1]{1,0:T(1,128)}, s32[1,1]{1,0:T(1,128)}, u32[]{:S(2)}, u32[]{:S(2)}) collective-permute-start(s32[1,1]{1,0:T(1,128)} %add.155), channel_id=1, source_target_pairs={{0,1},{1,2},{2,3},{3,4},{4,5},{5,6},{6,7},{7,8},{8,9},{9,10},{10,1... | collective-permute-start | bytes 20 | tf_op jit(solution)/shard_map/ppermute | solution.py:31
  73.3 45.7 %collective-permute-start.1 = (s32[1,1]{1,0:T(1,128)}, s32[1,1]{1,0:T(1,128)}, u32[]{:S(2)}, u32[]{:S(2)}) collective-permute-start(s32[1,1]{1,0:T(1,128)} %sub.157), channel_id=1, source_target_pairs={{0,1},{1,2},{2,3},{3,4},{4,5},{5,6},{6,7},{7,8},{8,9},{9,10},{10,1... | collective-permute-start | bytes 20 | tf_op jit(solution)/shard_map/ppermute | solution.py:31
  84.0 0.8 copy-start.15
  84.0 0.9 copy-start.16
  84.6 0.9 copy-start.23
  84.6 1.2 copy-start.24
  85.8 0.9 copy-start.9
  86.7 0.7 copy-start.19
  87.2 3.1 copy-start.3
  89.6 0.6 copy-start.7
  91.6 0.9 copy-start.10
  96.2 3.3 copy-start.11
  102.2 2.2 copy-start.8
  102.2 3.0 copy-start.17
  114.1 1.1 copy-start.6
  114.5 1.9 copy-start.13
  115.1 2.4 copy-start.2
  115.1 2.4 copy-start.5
  118.9 1.5 copy-start.4
  118.9 5.9 copy-start.22
  118.9 113.8 %copy-start.20 = (pred[12]{0:T(512)(128)(4,1)S(1)}, pred[12]{0:T(512)(128)(4,1)}, u32[]{:S(2)}) copy-start(pred[12]{0:T(512)(128)(4,1)} %get-tuple-element.127) | copy-start | bytes 40
  118.9 113.8 %copy-start.21 = (s32[12]{0:T(128)S(1)}, s32[12]{0:T(128)}, u32[]{:S(2)}) copy-start(s32[12]{0:T(128)} %get-tuple-element.128) | copy-start | bytes 148
  120.8 112.8 %collective-permute-start.2 = (bf16[1,24,4,576]{3,2,1,0:T(4,128)(2,1)S(1)}, bf16[1,24,4,576]{3,2,1,0:T(4,128)(2,1)S(1)}, u32[]{:S(2)}, u32[]{:S(2)}) collective-permute-start(bf16[1,24,4,576]{3,2,1,0:T(4,128)(2,1)S(1)} %reshape_reshape.4), channel_id=1, source_target_pairs={{0,1},{1,2},{2,3},{3,4},{4,5},{5,6},{6,7},{7,8},{8,9},{9,10},{10,1... | collective-permute-start | bytes 331784 | tf_op jit(solution)/shard_map/ppermute | solution.py:31
  599.7 2.3 copy-start.12
  602.0 1.1 copy-start.14
Sparse Core Ops, SparseCore 0:
  119.1 480.5 all-reduce.4
where the time goes:
time: 613 us; the launch traced here: 611 us
  waiting for transfers between devices  365 us (60%)
  blocking collectives  116 us (19%)
  local copies, waits for them, and re-layouts  36.7 us (6%)
  starting transfers between devices  21.9 us (4%)
  loops' own time  21.5 us (4%)
  matrix products  19.1 us (3%)
  other arithmetic  15.4 us (3%)
  between operations  15.2 us (2%)
    psum x1, waiting for transfers between devices, local(): lax.psum((grads[0], grads[1], grads[2], grads[3], grads[4]), ('img', 'uni...  365 us
    psum x1, blocking collectives, local(): lax.psum((grads[0], grads[1], grads[2], grads[3], grads[4]), ('img', 'uni...  108 us
    ppermute x4, starting transfers between devices, from_behind(): return lax.ppermute(block, axis, route)  21.8 us
    another operation x1, loops' own time, prefix(): return lax.fori_loop(0, peers, turn, start)  21.5 us
    dynamic_slice x32, local copies, waits for them, and re-layouts, turn(): new = combine(before, everything[k])  18.7 us
  transfers between devices with their start and end apart: 5, of which 1 were waited for; matrix products, arithmetic and copies ran while one was open for 11% of the time, Pallas kernels for 0%

commit v1 on v0

v1 whole, which is shorter than its diff:
```python
import functools
import math

import jax
import jax.numpy as jnp
from jax import lax
from jax.experimental import pallas as pl
from jax.experimental.pallas import tpu as pltpu
from jax.sharding import PartitionSpec as P

HEADS = 4
HEAD_DIM = 72
EPSILON = 1e-06
BF = jnp.bfloat16
F32 = jnp.float32
MESH = pl.DeviceIdType.MESH
TOK = 16
BLK = 128
LANES = 128
HALF = 2048
VMEM_LIMIT = 50 * 1024 * 1024


def nn(a, b):
    return lax.dot_general(a, b, (((1,), (0,)), ((), ())), preferred_element_type=F32)


def nt(a, b):
    return lax.dot_general(a, b, (((1,), (1,)), ((), ())), preferred_element_type=F32)


def tn(a, b):
    return lax.dot_general(a, b, (((0,), (0,)), ((), ())), preferred_element_type=F32)


def normalize(values):
    centred = values - jnp.mean(values, axis=-1, keepdims=True)
    inv_scale = lax.rsqrt(jnp.mean(centred * centred, axis=-1, keepdims=True) + EPSILON)
    return centred * inv_scale, inv_scale


def norm_back(grad_norm, normed_v, inv_scale):
    first = jnp.mean(grad_norm, axis=-1, keepdims=True)
    second = jnp.mean(grad_norm * normed_v, axis=-1, keepdims=True)
    return inv_scale * (grad_norm - first - normed_v * second)


def selection(shape, token_dim, shift, live):
    token = lax.broadcasted_iota(jnp.int32, shape, token_dim)
    row = lax.broadcasted_iota(jnp.int32, shape, 1 - token_dim)
    slot = token >> 4
    group = ((token >> 3) & 1) * 2 + ((token >> 1) & 1)
    hit = (row == (shift + slot) * 4 + group) & (slot < live)
    return jnp.where(hit, 0.25, 0.0).astype(BF)


def head_rows(block):
    lane = lax.broadcasted_iota(jnp.int32, (1, block.shape[1]), 1)
    parts = []
    for head in range(HEADS):
        mine = (lane >= head * HEAD_DIM) & (lane < (head + 1) * HEAD_DIM)
        parts.append(block * jnp.where(mine, 1.0, 0.0).astype(BF))
    return jnp.concatenate(parts, axis=0)


def heads_to_lanes(rows):
    return jnp.concatenate([rows[h * BLK : (h + 1) * BLK] for h in range(HEADS)], axis=1)


def gain_rows(total):
    row = lax.broadcasted_iota(jnp.int32, (32, LANES), 0)
    last = jnp.concatenate([total[:, 256:], jnp.zeros((1, 96), F32)], axis=1)
    out = jnp.where(row == 0, total[:, :128], 0.0)
    out = jnp.where(row == 1, total[:, 128:256], out)
    return jnp.where(row == 2, last, out).astype(BF)


def compute_kernel(
    live_ref, counts_ref, tokens_ref, cot_ref, next_ref, w_qkv_ref, w_out_ref, w_pool_ref, gain_one_ref, gain_two_ref,
    grad_tokens_ref, pooled_ref, g_ref, n_one_ref, n_two_ref, gr_ref, qkv_ref, mixed_ref, gqkv_ref, att_ref,
):
    rows, width = tokens_ref.shape
    me = lax.axis_index("unit")
    peers = counts_ref.shape[0]
    out_slots = cot_ref.shape[0] // 4
    factor = HEAD_DIM ** (-0.5)
    blocks = rows // BLK

    before = jnp.zeros((8, LANES), jnp.int32)
    for k in range(peers):
        before = before + jnp.where(k < me, counts_ref[k], 0)
    shift = before[0:1, :] - me * out_slots
    live = live_ref[0, 0]

    x = tokens_ref[...].astype(F32)
    n_one, p_one = normalize(x)
    n_one_ref[...] = n_one
    normed = (n_one * gain_one_ref[...]).astype(BF)
    qkv_ref[...] = nn(normed, w_qkv_ref[...]).astype(BF)

    same = (
        lax.broadcasted_iota(jnp.int32, (HEADS * BLK, BLK), 0) & (BLK - 1)
    ) >> 4 == lax.broadcasted_iota(jnp.int32, (HEADS * BLK, BLK), 1) >> 4
    for b in range(blocks):
        span = slice(b * BLK, (b + 1) * BLK)
        query = head_rows(qkv_ref[span, :width])
        scores = nt(query, qkv_ref[span, width : 2 * width]) * factor
        scores = jnp.where(same, scores, -1e30)
        e = jnp.exp(scores - jnp.max(scores, axis=-1, keepdims=True))
        att = e * (1.0 / jnp.sum(e, axis=-1, keepdims=True))
        att_ref[b] = att
        value = head_rows(qkv_ref[span, 2 * width :])
        mixed_ref[span, :] = nn(heads_to_lanes(att.astype(BF)), value).astype(BF)

    n_two, p_two = normalize(x + nn(mixed_ref[...], w_out_ref[...]))
    n_two_ref[...] = n_two
    y = n_two * gain_two_ref[...]
    high = y.astype(BF)
    low = (y - high.astype(F32)).astype(BF)
    ranked = 2 * 4 * out_slots
    gather = selection((ranked, rows), 1, before[0:1, 0:1] - me * out_slots, live)
    spread = selection((rows, ranked), 0, shift[:, :ranked], live)
    grouped = (nn(gather, high) + nn(gather, low)).astype(BF)
    pooled_ref[...] = nn(grouped, w_pool_ref[...]).astype(BF)

    cots = jnp.concatenate([cot_ref[...], next_ref[...]], axis=0)
    grad_pool = tn(grouped, cots).astype(BF)
    g_scaled = nt(nn(spread, cots).astype(BF), w_pool_ref[...])
    n_two = n_two_ref[...]
    g_ref[2016:2048, :] = gain_rows(jnp.sum(g_scaled * n_two, axis=0, keepdims=True))
    g_resid = norm_back(g_scaled * gain_two_ref[...], n_two, p_two)
    gr_ref[...] = g_resid
    resid_b = g_resid.astype(BF)
    grad_out = tn(mixed_ref[...], resid_b).astype(BF)
    for k in range(4):
        g_ref[width * k : width * (k + 1), :] = grad_pool[:, LANES * k : LANES * (k + 1)]
    g_ref[width * 4 : width * 5, :] = jnp.concatenate(
        [grad_pool[:, 512:576], grad_out[:, 256:288], jnp.zeros((width, 32), BF)], axis=1
    )
    g_ref[width * 5 : width * 6, :] = grad_out[:, :128]
    g_ref[width * 6 : width * 7, :] = grad_out[:, 128:256]

    mixed_ref[...] = nt(resid_b, w_out_ref[...]).astype(BF)
    for b in range(blocks):
        span = slice(b * BLK, (b + 1) * BLK)
        att = att_ref[b]
        g_mixed = head_rows(mixed_ref[span, :])
        g_att = nt(g_mixed, qkv_ref[span, 2 * width :])
        g_value = tn(att.astype(BF), g_mixed).astype(BF)
        g_scores = (att * (g_att - jnp.sum(g_att * att, axis=-1, keepdims=True)) * factor).astype(BF)
        g_query = nn(heads_to_lanes(g_scores), head_rows(qkv_ref[span, width : 2 * width])).astype(BF)
        g_key = tn(g_scores, head_rows(qkv_ref[span, :width])).astype(BF)
        gqkv_ref[span, :] = jnp.concatenate([g_query, g_key, g_value], axis=1)

    g_qkv = gqkv_ref[...]
    n_one = n_one_ref[...]
    normed = (n_one * gain_one_ref[...]).astype(BF)
    grad_qkv = tn(normed, g_qkv).astype(BF)
    for k in range(6):
        g_ref[HALF + width * k : HALF + width * (k + 1), :] = grad_qkv[:, LANES * k : LANES * (k + 1)]
    g_ref[HALF + width * 6 : HALF + width * 7, :] = jnp.concatenate(
        [grad_qkv[:, 768:864], jnp.zeros((width, 32), BF)], axis=1
    )
    g_normed = nt(g_qkv, w_qkv_ref[...])
    g_ref[HALF + 2016 : HALF + 2048, :] = gain_rows(jnp.sum(g_normed * n_one, axis=0, keepdims=True))
    g_input = norm_back(g_normed * gain_one_ref[...], n_one, p_one)
    grad_tokens_ref[...] = (gr_ref[...] + g_input).astype(BF)


def exchange_kernel(live_ref, cot_ref, counts_ref, next_ref, send_sem, count_sem, cot_sems):
    me = lax.axis_index("unit")
    peers = counts_ref.shape[0]
    barrier = pltpu.get_barrier_semaphore()
    for d in range(1, peers):
        pl.semaphore_signal(barrier, inc=1, device_id={"unit": lax.rem(me + d, peers)}, device_id_type=MESH)
    counts_ref[me] = jnp.full((8, LANES), live_ref[0, 0], jnp.int32)
    pl.semaphore_wait(barrier, peers - 1)
    shift = pltpu.make_async_remote_copy(
        src_ref=cot_ref, dst_ref=next_ref, send_sem=cot_sems.at[0], recv_sem=cot_sems.at[1],
        device_id={"unit": lax.rem(me + peers - 1, peers)}, device_id_type=MESH,
    )
    shift.start()
    for d in range(1, peers):
        pltpu.make_async_remote_copy(
            src_ref=counts_ref.at[me], dst_ref=counts_ref.at[me], send_sem=send_sem, recv_sem=count_sem,
            device_id={"unit": lax.rem(me + d, peers)}, device_id_type=MESH,
        ).start()
    others = counts_ref.at[pl.ds(0, peers - 1)]
    pltpu.make_async_copy(others, others, send_sem).wait()
    pltpu.make_async_copy(others, others, count_sem).wait()
    shift.wait()


def reduce_kernel(
    g_ref, pooled_ref, f_ref, prev_ref, r_one, s_ref, r_two, t_ref, r_three, w_ref, u_ref,
    pool_sems, one_send, one_recv, two_send, two_recv, three_send, three_recv, four_send, four_recv,
    five_send, five_recv, six_send, six_recv,
):
    me = lax.axis_index("unit")
    z = lax.axis_index("img")
    units = lax.axis_size("unit")
    nz = lax.axis_size("img")
    chips = units // 2
    core = lax.rem(me, 2)
    chip = me // 2
    half = HALF // 2
    piece = half // chips
    owners = nz // 2
    tile = 2 * piece // owners
    sibling = me + 1 - 2 * core
    other = lax.rem(me + units + 2 * core - 1, units)

    def plane(d):
        return lax.rem(chip + d, chips) * 2 + core

    barrier = pltpu.get_barrier_semaphore()
    pl.semaphore_signal(barrier, inc=1, device_id={"unit": sibling}, device_id_type=MESH)
    pl.semaphore_signal(barrier, inc=1, device_id={"unit": other}, device_id_type=MESH)
    for d in range(1, chips):
        pl.semaphore_signal(barrier, inc=1, device_id={"unit": plane(d)}, device_id_type=MESH)
    for d in range(1, nz):
        pl.semaphore_signal(barrier, inc=1, device_id={"img": lax.rem(z + d, nz)}, device_id_type=MESH)
    pl.semaphore_wait(barrier, chips + nz)

    firsts = []
    for part in range(2):
        copy = pltpu.make_async_remote_copy(
            src_ref=g_ref.at[pl.ds(pl.multiple_of(part * HALF + (1 - core) * half, half), half)],
            dst_ref=r_one.at[part], send_sem=one_send.at[part], recv_sem=one_recv.at[part],
            device_id={"unit": sibling}, device_id_type=MESH,
        )
        copy.start()
        firsts.append(copy)
    pooled_copy = pltpu.make_async_remote_copy(
        src_ref=pooled_ref.at[pl.ds(pooled_ref.shape[0] // 2, pooled_ref.shape[0] // 2)], dst_ref=prev_ref,
        send_sem=pool_sems.at[0], recv_sem=pool_sems.at[1],
        device_id={"unit": lax.rem(me + 1, units)}, device_id_type=MESH,
    )
    pooled_copy.start()

    for part in range(2):
        firsts[part].wait_recv()
        own = g_ref[pl.ds(pl.multiple_of(part * HALF + core * half, half), half), :]
        s_ref[part] = (own.astype(F32) + r_one[part].astype(F32)).astype(BF)
        for d in range(1, chips):
            pltpu.make_async_remote_copy(
                src_ref=s_ref.at[part, pl.ds(pl.multiple_of(lax.rem(chip + d, chips) * piece, piece), piece)],
                dst_ref=r_two.at[part, d], send_sem=two_send.at[part], recv_sem=two_recv.at[part],
                device_id={"unit": plane(d)}, device_id_type=MESH,
            ).start()
    for part in range(2):
        landed = r_two.at[part, pl.ds(1, chips - 1)]
        pltpu.make_async_copy(landed, landed, two_recv.at[part]).wait()
        total = s_ref[part, pl.ds(pl.multiple_of(chip * piece, piece), piece), :].astype(F32)
        for d in range(1, chips):
            total = total + r_two[part, d].astype(F32)
        t_ref[pl.ds(part * piece, piece), :] = total.astype(BF)

    for t in range(owners):
        owner = lax.rem(2 * t + core, nz)

        @pl.when(owner != z)
        def _():
            pltpu.make_async_remote_copy(
                src_ref=t_ref.at[pl.ds(t * tile, tile)], dst_ref=r_three.at[z], send_sem=three_send,
                recv_sem=three_recv, device_id={"img": owner}, device_id_type=MESH,
            ).start()

    owning = lax.rem(z, 2) == core
    mine = (z - lax.rem(z, 2)) // 2
    span = pl.ds(pl.multiple_of(mine * tile, tile), tile)

    @pl.when(owning)
    def _():
        r_three[z] = t_ref[span, :]
        landed = r_three.at[pl.ds(0, nz - 1)]
        pltpu.make_async_copy(landed, landed, three_recv).wait()
        total = r_three[0].astype(F32)
        for k in range(1, nz):
            total = total + r_three[k].astype(F32)
        u_ref[...] = total.astype(BF)
        for d in range(1, nz):
            pltpu.make_async_remote_copy(
                src_ref=u_ref, dst_ref=w_ref.at[span], send_sem=four_send,
                recv_sem=four_recv, device_id={"img": lax.rem(z + d, nz)}, device_id_type=MESH,
            ).start()
        w_ref[span, :] = u_ref[...]
        if owners > 1:
            rest = w_ref.at[pl.ds(0, (owners - 1) * tile)]
            pltpu.make_async_copy(rest, rest, four_recv).wait()
            pltpu.make_async_copy(rest, rest, three_send).wait()
        sent = r_three.at[pl.ds(0, nz - 1)]
        pltpu.make_async_copy(sent, sent, four_send).wait()

    @pl.when(jnp.logical_not(owning))
    def _():
        pltpu.make_async_copy(w_ref, w_ref, four_recv).wait()
        pltpu.make_async_copy(w_ref, w_ref, three_send).wait()

    chunk = 2 * piece

    def place(which_core, which_chip):
        return pl.ds(pl.multiple_of(which_core * HALF + which_chip * chunk, chunk), chunk)

    for d in range(1, chips):
        pltpu.make_async_remote_copy(
            src_ref=w_ref, dst_ref=f_ref.at[place(core, chip)], send_sem=five_send,
            recv_sem=five_recv.at[d], device_id={"unit": plane(d)}, device_id_type=MESH,
        ).start()
    f_ref[place(core, chip), :] = w_ref[...]
    for d in range(chips):
        source = lax.rem(chip + chips - d, chips)
        if d > 0:
            arrived = f_ref.at[place(core, source)]
            pltpu.make_async_copy(arrived, arrived, five_recv.at[d]).wait()
        pltpu.make_async_remote_copy(
            src_ref=f_ref.at[place(core, source)], dst_ref=f_ref.at[place(core, source)],
            send_sem=six_send, recv_sem=six_recv, device_id={"unit": sibling}, device_id_type=MESH,
        ).start()
    whole = f_ref.at[pl.ds(0, HALF)]
    pltpu.make_async_copy(whole, whole, six_send).wait()
    pltpu.make_async_copy(whole, whole, six_recv).wait()
    sent = f_ref.at[pl.ds(0, (chips - 1) * chunk)]
    pltpu.make_async_copy(sent, sent, five_send).wait()
    for part in range(2):
        firsts[part].wait_send()
        sent = s_ref.at[part, pl.ds(0, (chips - 1) * piece)]
        pltpu.make_async_copy(sent, sent, two_send.at[part]).wait()
    pooled_copy.wait()


def unpack_kernel(chips, scale, f_ref, pooled_ref, prev_ref, out_ref, qkv_ref, go_ref, pool_ref, one_ref, two_ref):
    piece = HALF // 2 // chips
    chunk = 2 * piece
    width = go_ref.shape[0]
    step = 32

    def rows32(part, row):
        half = HALF // 2
        core, rest = row // half, row % half
        at = core * HALF + rest // piece * chunk + part * piece + rest % piece
        return f_ref[at : at + step, :].astype(F32) * scale

    for k in range(7):
        for r in range(0, width, step):
            span = slice(r, r + step)
            early = rows32(0, width * k + r)
            late = rows32(1, width * k + r)
            if k < 6:
                qkv_ref[span, LANES * k : LANES * (k + 1)] = late
            else:
                qkv_ref[span, 768:864] = late[:, :96]
            if k < 4:
                pool_ref[span, LANES * k : LANES * (k + 1)] = early
            elif k == 4:
                pool_ref[span, 512:576] = early[:, :64]
                go_ref[span, 256:288] = early[:, 64:96]
            else:
                go_ref[span, LANES * (k - 5) : LANES * (k - 4)] = early
    for part, ref in ((0, two_ref), (1, one_ref)):
        last = rows32(part, 2016)
        ref[...] = jnp.concatenate([last[0:1], last[1:2], last[2:3, :32]], axis=1)
    own = pooled_ref[: out_ref.shape[0], :]
    out_ref[...] = own + prev_ref[...]


def full(count):
    return [pl.BlockSpec(memory_space=pltpu.VMEM)] * count


def local(tokens, live, cotangent, w_qkv, w_out, w_pool, gain_one, gain_two):
    img_dev, slots, token_count, width = tokens.shape
    out_slots, out_width = cotangent.shape[1], cotangent.shape[3]
    units, nz = lax.axis_size("unit"), lax.axis_size("img")
    chips = units // 2
    rows = slots * token_count
    crows = out_slots * 4
    piece = HALF // 2 // chips
    tile = 2 * piece // (nz // 2)
    cot = cotangent.reshape(crows, out_width)
    tok = tokens.reshape(rows, width)
    dma, smem = pltpu.SemaphoreType.DMA, pl.BlockSpec(memory_space=pltpu.SMEM)

    def sd(shape, dtype):
        return jax.ShapeDtypeStruct(shape, dtype)

    counts, next_cot = pl.pallas_call(
        exchange_kernel,
        out_shape=(sd((units, 8, LANES), jnp.int32), sd((crows, out_width), BF)),
        in_specs=[smem] + full(1),
        out_specs=full(2),
        scratch_shapes=[dma, dma, dma((2,))],
        compiler_params=pltpu.CompilerParams(collective_id=0, has_side_effects=True, vmem_limit_bytes=VMEM_LIMIT),
        name="exchange",
    )(live, cot)

    grad_tokens, pooled, g = pl.pallas_call(
        compute_kernel,
        out_shape=(sd((rows, width), BF), sd((2 * crows, out_width), BF), sd((2 * HALF, LANES), BF)),
        in_specs=[smem] + full(9),
        out_specs=full(3),
        scratch_shapes=[
            pltpu.VMEM((rows, width), F32),
            pltpu.VMEM((rows, width), F32),
            pltpu.VMEM((rows, width), F32),
            pltpu.VMEM((rows, 3 * width), BF),
            pltpu.VMEM((rows, width), BF),
            pltpu.VMEM((rows, 3 * width), BF),
            pltpu.VMEM((rows // BLK, HEADS * BLK, BLK), F32),
        ],
        compiler_params=pltpu.CompilerParams(vmem_limit_bytes=VMEM_LIMIT),
        name="compute",
    )(live, counts, tok, cot, next_cot, w_qkv, w_out, w_pool, gain_one[None], gain_two[None])

    f, prev = pl.pallas_call(
        reduce_kernel,
        out_shape=(sd((2 * HALF, LANES), BF), sd((crows, out_width), BF)),
        in_specs=full(2),
        out_specs=full(2),
        scratch_shapes=[
            pltpu.VMEM((2, HALF // 2, LANES), BF),
            pltpu.VMEM((2, HALF // 2, LANES), BF),
            pltpu.VMEM((2, chips, piece, LANES), BF),
            pltpu.VMEM((2 * piece, LANES), BF),
            pltpu.VMEM((nz, tile, LANES), BF),
            pltpu.VMEM((2 * piece, LANES), BF),
            pltpu.VMEM((tile, LANES), BF),
            dma((2,)), dma((2,)), dma((2,)), dma((2,)), dma((2,)), dma, dma, dma, dma,
            dma, dma((chips,)), dma, dma,
        ],
        compiler_params=pltpu.CompilerParams(collective_id=1, has_side_effects=True, vmem_limit_bytes=VMEM_LIMIT),
        name="reduce",
    )(g, pooled)

    scale = 1.0 / math.sqrt(img_dev * nz * out_slots * units)
    out, grad_qkv, grad_out, grad_pool, one, two = pl.pallas_call(
        functools.partial(unpack_kernel, chips, scale),
        out_shape=(
            sd((crows, out_width), BF), sd((width, 3 * width), F32), sd((width, width), F32),
            sd((width, out_width), F32), sd((1, width), F32), sd((1, width), F32),
        ),
        in_specs=full(3),
        out_specs=full(6),
        compiler_params=pltpu.CompilerParams(vmem_limit_bytes=VMEM_LIMIT),
        name="unpack",
    )(f, pooled, prev)
    return (
        out.reshape(cotangent.shape), grad_tokens.reshape(tokens.shape),
        grad_qkv, grad_out, grad_pool, one.reshape(width), two.reshape(width),
    )


def solution(mesh):
    return jax.shard_map(
        local,
        mesh=mesh,
        in_specs=(
            P("img", "unit", None, None), P("img", "unit"), P("img", "unit", None, None),
            P(), P(), P(), P(), P(),
        ),
        out_specs=(P("img", "unit", None, None), P("img", "unit", None, None), P(), P(), P(), P(), P()),
        check_vma=False,
    )
```

time: 613 us -> 80.3 us (0.13)
  waiting for transfers between devices: 365 us -> 0 us
  blocking collectives: 116 us -> 0 us
  Pallas kernels: 0 us -> 71.3 us
  local copies, waits for them, and re-layouts: 36.7 us -> 6.11 us
  starting transfers between devices: 21.9 us -> 0 us
  loops' own time: 21.5 us -> 0 us
  matrix products: 19.1 us -> 0 us
  other arithmetic: 15.4 us -> 1.19 us
  between operations: 15.2 us -> 1.34 us
    psum x1 -> x0, waiting for transfers between devices: 365 us -> none  [local(): lax.psum((grads[0], grads[1], grads[2], grads[3], grads[4]), ('img', 'uni...]
    psum x1 -> x0, blocking collectives: 108 us -> none  [local(): lax.psum((grads[0], grads[1], grads[2], grads[3], grads[4]), ('img', 'uni...]
    pallas_call x0 -> x4, Pallas kernels: none -> 71.3 us  [the longest x1 45.7 us: local(): pl.pallas_call(reduce_kernel, out_shape=(sd((2 * HALF, LANES), BF), sd((c...]
    ppermute x4 -> x0, starting transfers between devices: 21.8 us -> none  [from_behind(): return lax.ppermute(block, axis, route)]
    another operation x1 -> x0, loops' own time: 21.5 us -> none  [prefix(): return lax.fori_loop(0, peers, turn, start)]
    dynamic_slice x32 -> x0, local copies, waits for them, and re-layouts: 18.7 us -> none  [turn(): new = combine(before, everything[k])]
    dot_general x18 -> x0, matrix products: 18.6 us -> none  [the longest x5 9.77 us: mult(): return jnp.einsum(form, left, right, preferred_element_type=jnp.float32)]
    unnamed x1 -> x0, blocking collectives: 8.07 us -> none
  transfers between devices with their start and end apart: 5 -> 0, of which waited for: 1 -> 0; matrix products, arithmetic and copies ran while one was open for 11% -> 0% of each run, Pallas kernels for 0% -> 0%
where the time goes in v1:
time: 80.3 us; the launch traced here: 80 us
  Pallas kernels  71.3 us (89%)
  local copies, waits for them, and re-layouts  6.11 us (8%)
  between operations  1.34 us (2%)
  other arithmetic  1.19 us (1%)
    pallas_call x1, Pallas kernels, local(): pl.pallas_call(reduce_kernel, out_shape=(sd((2 * HALF, LANES), BF), sd((c...  45.7 us
    pallas_call x1, Pallas kernels, local(): pl.pallas_call(exchange_kernel, out_shape=(sd((units, 8, LANES), jnp.int3...  15.3 us
    pallas_call x1, Pallas kernels, local(): pl.pallas_call(compute_kernel, out_shape=(sd((rows, width), BF), sd((2 *...  8.89 us
    unnamed x12, local copies, waits for them, and re-layouts  4.6 us

profile of v1, /device:TPU:1, one launch (start us, length us, event | category | flops | bytes accessed | tf_op | source)
XLA Modules:
  0.0 80.0 jit_solution(8472818680348385049)
XLA Ops:
  0.6 0.0 copy-start.4
  1.3 0.0 copy-done.4
  1.3 0.0 copy-start.5
  1.3 0.7 copy-done.5
  2.0 0.9 %reshape.32.cot_ref = bf16[48,576]{1,0:T(8,128)(2,1)S(1)} reshape(bf16[1,12,4,576]{3,2,1,0:T(4,128)(2,1)} %param.10) | data formatting | bytes 110592 | tf_op jit(solution)/shard_map/reshape | solution.py:380
  2.9 15.3 %exchange.1 = (s32[32,8,128]{2,1,0:T(8,128)S(1)}, bf16[48,576]{1,0:T(8,128)(2,1)S(1)}) custom-call(s32[1,1]{1,0:T(1,128)S(6)} %copy.15.live_ref, bf16[48,576]{1,0:T(8,128)(2,1)S(1)} %reshape.32.cot_ref), custom_call_target="tpu_custom_call" | custom-call | tf_op jit(solution)/shard_map/exchange/pallas_call | solution.py:387
  18.2 0.0 copy-start
  18.2 1.0 %copy-done = bf16[288,864]{1,0:T(8,128)(2,1)S(1)} copy-done((bf16[288,864]{1,0:T(8,128)(2,1)S(1)}, bf16[288,864]{1,0:T(8,128)(2,1)}, u32[]{:S(2)}) %copy-start) | copy-done | bytes 497688
  19.2 0.0 copy-start.1
  19.2 1.0 %copy-done.1 = bf16[288,576]{1,0:T(8,128)(2,1)S(1)} copy-done((bf16[288,576]{1,0:T(8,128)(2,1)S(1)}, bf16[288,576]{1,0:T(8,128)(2,1)}, u32[]{:S(2)}) %copy-start.1) | copy-done | bytes 331800
  20.2 0.0 copy-start.2
  20.2 1.0 %copy-done.2 = bf16[1,24,16,288]{3,2,1,0:T(8,128)(2,1)S(1)} copy-done((bf16[1,24,16,288]{3,2,1,0:T(8,128)(2,1)S(1)}, bf16[1,24,16,288]{3,2,1,0:T(8,128)(2,1)}, u32[]{:S(2)}) %copy-start.2) | copy-done | bytes 221208
  21.2 0.0 copy-start.3
  21.2 0.9 %copy-done.3 = bf16[288,288]{1,0:T(8,128)(2,1)S(1)} copy-done((bf16[288,288]{1,0:T(8,128)(2,1)S(1)}, bf16[288,288]{1,0:T(8,128)(2,1)}, u32[]{:S(2)}) %copy-start.3) | copy-done | bytes 165912
  22.1 8.9 %compute.1 = (bf16[384,288]{1,0:T(8,128)(2,1)}, bf16[96,576]{1,0:T(8,128)(2,1)S(1)}, bf16[4096,128]{1,0:T(8,128)(2,1)S(1)}) custom-call(s32[1,1]{1,0:T(1,128)S(6)} %copy.15.live_ref, s32[32,8,128]{2,1,0:T(8,128)S(1)} %get-tuple-element.20.counts_ref, bf16[384,288]{1,0:T(8,128)(2,1)S(1)} %bitcast.2, bf16[48,576]{1,0:T(8,128)(2,1)S(1)} %reshape.32.cot_ref, ...), custom_call_target="tpu_custom_call" | custom-call | tf_op jit(solution)/shard_map/compute/pallas_call | solution.py:397
  31.0 45.7 %reduce.3 = (bf16[4096,128]{1,0:T(8,128)(2,1)S(1)}, bf16[48,576]{1,0:T(8,128)(2,1)S(1)}) custom-call(bf16[4096,128]{1,0:T(8,128)(2,1)S(1)} %get-tuple-element.22.g_ref, bf16[96,576]{1,0:T(8,128)(2,1)S(1)} %get-tuple-element.23.pooled_ref), custom_call_target="tpu_custom_call" | custom-call | tf_op jit(solution)/shard_map/reduce/pallas_call | solution.py:415
  76.7 1.5 %unpack.1 = (bf16[48,576]{1,0:T(8,128)(2,1)S(1)}, f32[288,864]{1,0:T(8,128)}, f32[288,288]{1,0:T(8,128)}, f32[288,576]{1,0:T(8,128)}, f32[1,288]{1,0:T(1,128)S(1)}, /*index=5*/f32[1,288]{1,0:T(1,128)S(1)}) custom-call(bf16[4096,128]{1,0:T(8,128)(2,1)S(1)} %get-tuple-element.24.f_ref, bf16[96,576]{1,0:T(8,128)(2,1)S(1)} %get-tuple-element.23.pooled_ref, ...), custom_call_target="tpu_custom_call" | custom-call | tf_op jit(solution)/shard_map/unpack/pallas_call | solution.py:436
  78.1 0.6 reshape.34
  78.8 0.6 reduce.1
  79.4 0.6 reduce.2
  (2 shorter events, 0.0 us)
Async XLA Ops:
  0.6 0.7 copy-start.4
  1.3 0.7 copy-start.5
  18.2 1.0 %copy-start = (bf16[288,864]{1,0:T(8,128)(2,1)S(1)}, bf16[288,864]{1,0:T(8,128)(2,1)}, u32[]{:S(2)}) copy-start(bf16[288,864]{1,0:T(8,128)(2,1)} %w_qkv_ref.1) | copy-start | bytes 1492996
  19.2 1.0 %copy-start.1 = (bf16[288,576]{1,0:T(8,128)(2,1)S(1)}, bf16[288,576]{1,0:T(8,128)(2,1)}, u32[]{:S(2)}) copy-start(bf16[288,576]{1,0:T(8,128)(2,1)} %w_pool_ref.1) | copy-start | bytes 995332
  20.2 1.0 %copy-start.2 = (bf16[1,24,16,288]{3,2,1,0:T(8,128)(2,1)S(1)}, bf16[1,24,16,288]{3,2,1,0:T(8,128)(2,1)}, u32[]{:S(2)}) copy-start(bf16[1,24,16,288]{3,2,1,0:T(8,128)(2,1)} %param.8) | copy-start | bytes 663556
  21.2 0.9 %copy-start.3 = (bf16[288,288]{1,0:T(8,128)(2,1)S(1)}, bf16[288,288]{1,0:T(8,128)(2,1)}, u32[]{:S(2)}) copy-start(bf16[288,288]{1,0:T(8,128)(2,1)} %w_out_ref.1) | copy-start | bytes 497668

commit v2 on v1

v2 whole, which is shorter than its diff:
```python
import functools
import math

import jax
import jax.numpy as jnp
from jax import lax
from jax.experimental import pallas as pl
from jax.experimental.pallas import tpu as pltpu
from jax.sharding import PartitionSpec as P

HEADS = 4
HEAD_DIM = 72
EPSILON = 1e-06
BF = jnp.bfloat16
F32 = jnp.float32
MESH = pl.DeviceIdType.MESH
TOK = 16
BLK = 128
LANES = 128
HALF = 2048
AROUND = {1: (0,), 2: (1, 0), 4: (2, 1, 3, 0)}
VMEM_LIMIT = 62 * 1024 * 1024


def nn(a, b):
    return lax.dot_general(a, b, (((1,), (0,)), ((), ())), preferred_element_type=F32)


def nt(a, b):
    return lax.dot_general(a, b, (((1,), (1,)), ((), ())), preferred_element_type=F32)


def tn(a, b):
    return lax.dot_general(a, b, (((0,), (0,)), ((), ())), preferred_element_type=F32)


def normalize(values):
    centred = values - jnp.mean(values, axis=-1, keepdims=True)
    inv_scale = lax.rsqrt(jnp.mean(centred * centred, axis=-1, keepdims=True) + EPSILON)
    return centred * inv_scale, inv_scale


def norm_back(grad_norm, normed_v, inv_scale):
    first = jnp.mean(grad_norm, axis=-1, keepdims=True)
    second = jnp.mean(grad_norm * normed_v, axis=-1, keepdims=True)
    return inv_scale * (grad_norm - first - normed_v * second)


def selection(shape, token_dim, shift, live):
    token = lax.broadcasted_iota(jnp.int32, shape, token_dim)
    row = lax.broadcasted_iota(jnp.int32, shape, 1 - token_dim)
    slot = token >> 4
    group = ((token >> 3) & 1) * 2 + ((token >> 1) & 1)
    hit = (row == (shift + slot) * 4 + group) & (slot < live)
    return jnp.where(hit, 0.25, 0.0).astype(BF)


def head_rows(block):
    lane = lax.broadcasted_iota(jnp.int32, (1, block.shape[1]), 1)
    parts = []
    for head in range(HEADS):
        mine = (lane >= head * HEAD_DIM) & (lane < (head + 1) * HEAD_DIM)
        parts.append(block * jnp.where(mine, 1.0, 0.0).astype(BF))
    return jnp.concatenate(parts, axis=0)


def heads_to_lanes(rows):
    return jnp.concatenate([rows[h * BLK : (h + 1) * BLK] for h in range(HEADS)], axis=1)


def gain_rows(total):
    row = lax.broadcasted_iota(jnp.int32, (32, LANES), 0)
    last = jnp.concatenate([total[:, 256:], jnp.zeros((1, 96), F32)], axis=1)
    out = jnp.where(row == 0, total[:, :128], 0.0)
    out = jnp.where(row == 1, total[:, 128:256], out)
    return jnp.where(row == 2, last, out).astype(BF)


def main_kernel(
    live_ref, tok_hbm, cot_hbm, w_qkv_hbm, w_out_hbm, w_pool_hbm, gain_one_hbm, gain_two_hbm,
    f_ref, pooled_out, grad_tokens_ref,
    tok_ref, cot_ref, w_qkv_ref, w_out_ref, w_pool_ref, gain_one_ref, gain_two_ref,
    counts_ref, cots_ref, pooled_ref, prev_ref, g_ref, n_one_ref, n_two_ref, gr_ref, qkv_ref, mixed_ref, gqkv_ref,
    att_ref, r_one, s_ref, r_two, t_ref, r_three, u_ref, w_ref,
    in_sems, count_sems, cot_sems, pool_sems, one_send, one_recv, two_send, two_recv, three_send, three_recv,
    four_send, four_recv, five_send, five_recv, six_send, six_recv,
):
    rows, width = tok_ref.shape
    crows = cots_ref.shape[0] // 2
    out_slots = crows // 4
    factor = HEAD_DIM ** (-0.5)
    blocks = rows // BLK
    me = lax.axis_index("unit")
    z = lax.axis_index("img")
    units = lax.axis_size("unit")
    nz = lax.axis_size("img")
    chips = units // 2
    nx = min(4, chips)
    ny = chips // nx
    core = lax.rem(me, 2)
    chip = me // 2
    chip_x, chip_y = lax.rem(chip, nx), chip // nx
    half = HALF // 2
    piece = half // chips
    tile = piece // 4
    sibling = me + 1 - 2 * core
    plane = [(dx, dy) for dx in AROUND[nx] for dy in AROUND[ny]][:-1]

    def chip_at(dx, dy):
        return lax.rem(chip_y + dy, ny) * nx + lax.rem(chip_x + dx, nx)

    def fetch(k, source, target):
        copy = pltpu.make_async_copy(source, target, in_sems.at[k])
        copy.start()
        return copy

    def push(source, target, send, recv, **where):
        copy = pltpu.make_async_remote_copy(
            src_ref=source, dst_ref=target, send_sem=send, recv_sem=recv, device_id=where, device_id_type=MESH
        )
        copy.start()
        return copy

    def drain(ref, sem):
        pltpu.make_async_copy(ref, ref, sem).wait()

    get_tok = fetch(0, tok_hbm, tok_ref)
    get_gain_one = fetch(1, gain_one_hbm, gain_one_ref)
    get_w_qkv = fetch(2, w_qkv_hbm, w_qkv_ref)
    get_cot = fetch(3, cot_hbm, cot_ref)
    get_w_out = fetch(4, w_out_hbm, w_out_ref)
    get_gain_two = fetch(5, gain_two_hbm, gain_two_ref)
    get_w_pool = fetch(6, w_pool_hbm, w_pool_ref)

    barrier = pltpu.get_barrier_semaphore()
    for d in range(1, nz):
        pl.semaphore_signal(barrier, inc=1, device_id={"img": lax.rem(z + d, nz)}, device_id_type=MESH)
    for d in range(1, units):
        pl.semaphore_signal(barrier, inc=1, device_id={"unit": lax.rem(me + d, units)}, device_id_type=MESH)

    def half_of(part, which):
        return pl.ds(pl.multiple_of(part * HALF + which * half, half), half)

    def pair_send(part):
        push(g_ref.at[half_of(part, 1 - core)], r_one.at[part], one_send.at[part], one_recv.at[part], unit=sibling)

    def pair_add(part):
        drain(r_one.at[part], one_recv.at[part])
        own = g_ref[half_of(part, core), :]
        s_ref[part] = (own.astype(F32) + r_one[part].astype(F32)).astype(BF)
        for k, (dx, dy) in enumerate(plane):
            there = chip_at(dx, dy)
            push(
                s_ref.at[part, pl.ds(pl.multiple_of(there * piece, piece), piece)], r_two.at[part, k],
                two_send.at[part], two_recv.at[part], unit=there * 2 + core,
            )

    def plane_add(part):
        drain(r_two.at[part], two_recv.at[part])
        total = s_ref[part, pl.ds(pl.multiple_of(chip * piece, piece), piece), :].astype(F32)
        for k in range(chips - 1):
            total = total + r_two[part, k].astype(F32)
        t_ref[part] = total.astype(BF)
        for d in range(1, nz):
            there = lax.rem(z + d, nz)
            push(
                t_ref.at[part, pl.ds(pl.multiple_of(lax.rem(there, 4) * tile, tile), tile)], r_three.at[part, z],
                three_send.at[part], three_recv.at[part], img=there,
            )
        r_three[part, z] = t_ref[part, pl.ds(pl.multiple_of(lax.rem(z, 4) * tile, tile), tile), :]

    mine = pl.ds(pl.multiple_of(lax.rem(z, 4) * tile, tile), tile)

    def line_add(part):
        drain(r_three.at[part, pl.ds(0, nz - 1)], three_recv.at[part])
        total = r_three[part, 0].astype(F32)
        for k in range(1, nz):
            total = total + r_three[part, k].astype(F32)
        u_ref[part] = total.astype(BF)
        for d in (2, 1, nz - 1):
            push(u_ref.at[part], w_ref.at[part, mine], four_send.at[part], four_recv.at[part], img=lax.rem(z + d, nz))
        w_ref[part, mine, :] = u_ref[part]

    def place(part, which_core, which_chip):
        return pl.ds(pl.multiple_of(part * HALF + which_core * half + which_chip * piece, piece), piece)

    def plane_spread(part):
        drain(w_ref.at[part, pl.ds(0, 3 * tile)], four_recv.at[part])
        here = place(part, core, chip)
        for k, (dx, dy) in enumerate(plane):
            push(
                w_ref.at[part], f_ref.at[here], five_send.at[part], five_recv.at[part, k],
                unit=chip_at(dx, dy) * 2 + core,
            )
        f_ref[here, :] = w_ref[part]
        push(w_ref.at[part], f_ref.at[here], six_send.at[part], six_recv.at[part], unit=sibling)

    def pair_spread(part):
        for k, (dx, dy) in reversed(list(enumerate(plane))):
            there = place(part, core, chip_at(nx - dx, ny - dy))
            drain(f_ref.at[there], five_recv.at[part, k])
            push(f_ref.at[there], f_ref.at[there], six_send.at[part], six_recv.at[part], unit=sibling)

    get_tok.wait()
    get_gain_one.wait()
    n_one, p_one = normalize(tok_ref[...].astype(F32))
    n_one_ref[...] = n_one
    normed = (n_one * gain_one_ref[...]).astype(BF)
    get_w_qkv.wait()
    qkv_ref[...] = nn(normed, w_qkv_ref[...]).astype(BF)

    same = (
        lax.broadcasted_iota(jnp.int32, (HEADS * BLK, BLK), 0) & (BLK - 1)
    ) >> 4 == lax.broadcasted_iota(jnp.int32, (HEADS * BLK, BLK), 1) >> 4
    for b in range(blocks):
        span = slice(b * BLK, (b + 1) * BLK)
        query = head_rows(qkv_ref[span, :width])
        scores = nt(query, qkv_ref[span, width : 2 * width]) * factor
        scores = jnp.where(same, scores, -1e30)
        e = jnp.exp(scores - jnp.max(scores, axis=-1, keepdims=True))
        att = e * (1.0 / jnp.sum(e, axis=-1, keepdims=True))
        att_ref[b] = att
        value = head_rows(qkv_ref[span, 2 * width :])
        mixed_ref[span, :] = nn(heads_to_lanes(att.astype(BF)), value).astype(BF)

    get_cot.wait()
    cots_ref[:crows, :] = cot_ref[...].reshape(crows, cots_ref.shape[1])
    counts_ref[me] = jnp.full((8, LANES), live_ref[0, 0], jnp.int32)
    pl.semaphore_wait(barrier, nz + units - 2)
    for d in range(1, units):
        push(counts_ref.at[me], counts_ref.at[me], count_sems.at[0], count_sems.at[1], unit=lax.rem(me + d, units))
    cot_copy = push(
        cots_ref.at[pl.ds(0, crows)], cots_ref.at[pl.ds(crows, crows)], cot_sems.at[0], cot_sems.at[1],
        unit=lax.rem(me + units - 1, units),
    )

    get_w_out.wait()
    get_gain_two.wait()
    n_two, p_two = normalize(tok_ref[...].astype(F32) + nn(mixed_ref[...], w_out_ref[...]))
    n_two_ref[...] = n_two
    y = n_two * gain_two_ref[...]
    high = y.astype(BF)
    low = (y - high.astype(F32)).astype(BF)

    get_w_pool.wait()
    others = counts_ref.at[pl.ds(0, units - 1)]
    drain(others, count_sems.at[1])
    before = jnp.zeros((8, LANES), jnp.int32)
    for k in range(units):
        before = before + jnp.where(k < me, counts_ref[k], 0)
    shift = before[0:1, :] - me * out_slots
    live = live_ref[0, 0]
    ranked = 2 * crows
    gather = selection((ranked, rows), 1, shift[:, 0:1], live)
    spread = selection((rows, ranked), 0, shift[:, :ranked], live)
    grouped = (nn(gather, high) + nn(gather, low)).astype(BF)
    pooled_ref[...] = nn(grouped, w_pool_ref[...]).astype(BF)
    pooled_copy = push(
        pooled_ref.at[pl.ds(crows, crows)], prev_ref, pool_sems.at[0], pool_sems.at[1],
        unit=lax.rem(me + 1, units),
    )

    cot_copy.wait_recv()
    cots = cots_ref[...]
    grad_pool = tn(grouped, cots).astype(BF)
    g_scaled = nt(nn(spread, cots).astype(BF), w_pool_ref[...])
    n_two = n_two_ref[...]
    g_ref[2016:2048, :] = gain_rows(jnp.sum(g_scaled * n_two, axis=0, keepdims=True))
    g_resid = norm_back(g_scaled * gain_two_ref[...], n_two, p_two)
    gr_ref[...] = g_resid
    resid_b = g_resid.astype(BF)
    grad_out = tn(mixed_ref[...], resid_b).astype(BF)
    for k in range(4):
        g_ref[width * k : width * (k + 1), :] = grad_pool[:, LANES * k : LANES * (k + 1)]
    g_ref[width * 4 : width * 5, :] = jnp.concatenate(
        [grad_pool[:, 512:576], grad_out[:, 256:288], jnp.zeros((width, 32), BF)], axis=1
    )
    g_ref[width * 5 : width * 6, :] = grad_out[:, :128]
    g_ref[width * 6 : width * 7, :] = grad_out[:, 128:256]
    pair_send(0)

    mixed_ref[...] = nt(resid_b, w_out_ref[...]).astype(BF)
    for b in range(blocks):
        span = slice(b * BLK, (b + 1) * BLK)
        att = att_ref[b]
        g_mixed = head_rows(mixed_ref[span, :])
        g_att = nt(g_mixed, qkv_ref[span, 2 * width :])
        g_value = tn(att.astype(BF), g_mixed).astype(BF)
        g_scores = (att * (g_att - jnp.sum(g_att * att, axis=-1, keepdims=True)) * factor).astype(BF)
        g_query = nn(heads_to_lanes(g_scores), head_rows(qkv_ref[span, width : 2 * width])).astype(BF)
        g_key = tn(g_scores, head_rows(qkv_ref[span, :width])).astype(BF)
        gqkv_ref[span, :] = jnp.concatenate([g_query, g_key, g_value], axis=1)
        if b == blocks - 2:
            pair_add(0)

    g_qkv = gqkv_ref[...]
    n_one = n_one_ref[...]
    normed = (n_one * gain_one_ref[...]).astype(BF)
    grad_qkv = tn(normed, g_qkv).astype(BF)
    for k in range(6):
        g_ref[HALF + width * k : HALF + width * (k + 1), :] = grad_qkv[:, LANES * k : LANES * (k + 1)]
    g_ref[HALF + width * 6 : HALF + width * 7, :] = jnp.concatenate(
        [grad_qkv[:, 768:864], jnp.zeros((width, 32), BF)], axis=1
    )
    g_normed = nt(g_qkv, w_qkv_ref[...])
    g_ref[HALF + 2016 : HALF + 2048, :] = gain_rows(jnp.sum(g_normed * n_one, axis=0, keepdims=True))
    pair_send(1)
    g_input = norm_back(g_normed * gain_one_ref[...], n_one, p_one)
    grad_tokens_ref[...] = (gr_ref[...] + g_input).astype(BF)

    pair_add(1)
    plane_add(0)
    pooled_copy.wait_recv()
    pooled_out[...] = pooled_ref[:crows, :] + prev_ref[...]
    plane_add(1)
    line_add(0)
    plane_spread(0)
    line_add(1)
    plane_spread(1)
    pair_spread(0)
    pair_spread(1)

    for part in range(2):
        drain(g_ref.at[pl.ds(0, half)], one_send.at[part])
        drain(r_two.at[part], two_send.at[part])
        drain(r_three.at[part, pl.ds(0, nz - 1)], three_send.at[part])
        drain(w_ref.at[part, pl.ds(0, 3 * tile)], four_send.at[part])
        drain(f_ref.at[pl.ds(0, half - piece)], five_send.at[part])
        drain(f_ref.at[pl.ds(0, half)], six_send.at[part])
        drain(f_ref.at[pl.ds(0, half)], six_recv.at[part])
    drain(others, count_sems.at[0])
    cot_copy.wait_send()
    pooled_copy.wait_send()


def unpack_kernel(
    scale, f_ref, pooled_ref, tok_ref, out_ref, grad_tokens_ref, qkv_ref, go_ref, pool_ref, one_ref, two_ref
):
    width = go_ref.shape[0]

    def rows(start, count):
        return f_ref[start : start + count, :].astype(F32) * scale

    for k in range(7):
        early = rows(width * k, width)
        late = rows(HALF + width * k, width)
        if k < 6:
            qkv_ref[:, LANES * k : LANES * (k + 1)] = late
        else:
            qkv_ref[:, 768:864] = late[:, :96]
        if k < 4:
            pool_ref[:, LANES * k : LANES * (k + 1)] = early
        elif k == 4:
            pool_ref[:, 512:576] = early[:, :64]
            go_ref[:, 256:288] = early[:, 64:96]
        else:
            go_ref[:, LANES * (k - 5) : LANES * (k - 4)] = early
    for start, ref in ((2016, two_ref), (HALF + 2016, one_ref)):
        last = rows(start, 32)
        ref[...] = jnp.concatenate([last[0:1], last[1:2], last[2:3, :32]], axis=1).reshape(ref.shape)
    out_ref[...] = pooled_ref[...].reshape(out_ref.shape)
    grad_tokens_ref[...] = tok_ref[...]


def whole(count, space=pltpu.VMEM):
    return [pl.BlockSpec(memory_space=space)] * count


def local(tokens, live, cotangent, w_qkv, w_out, w_pool, gain_one, gain_two):
    img_dev, slots, token_count, width = tokens.shape
    out_slots, out_width = cotangent.shape[1], cotangent.shape[3]
    units, nz = lax.axis_size("unit"), lax.axis_size("img")
    chips = units // 2
    rows = slots * token_count
    crows = out_slots * 4
    piece = HALF // 2 // chips
    dma, vmem = pltpu.SemaphoreType.DMA, pltpu.VMEM

    def sd(shape, dtype):
        return jax.ShapeDtypeStruct(shape, dtype)

    f, pooled, grad_tok = pl.pallas_call(
        main_kernel,
        out_shape=(sd((2 * HALF, LANES), BF), sd((crows, out_width), BF), sd((rows, width), BF)),
        in_specs=[pl.BlockSpec(memory_space=pltpu.SMEM)] + whole(7, pltpu.HBM),
        out_specs=whole(3),
        scratch_shapes=[
            vmem((rows, width), BF),
            vmem((out_slots, 4, out_width), BF),
            vmem(w_qkv.shape, BF),
            vmem(w_out.shape, BF),
            vmem(w_pool.shape, BF),
            vmem(gain_one.shape, F32),
            vmem(gain_two.shape, F32),
            vmem((units, 8, LANES), jnp.int32),
            vmem((2 * crows, out_width), BF),
            vmem((2 * crows, out_width), BF),
            vmem((crows, out_width), BF),
            vmem((2 * HALF, LANES), BF),
            vmem((rows, width), F32),
            vmem((rows, width), F32),
            vmem((rows, width), F32),
            vmem((rows, 3 * width), BF),
            vmem((rows, width), BF),
            vmem((rows, 3 * width), BF),
            vmem((rows // BLK, HEADS * BLK, BLK), F32),
            vmem((2, HALF // 2, LANES), BF),
            vmem((2, HALF // 2, LANES), BF),
            vmem((2, chips - 1, piece, LANES), BF),
            vmem((2, piece, LANES), BF),
            vmem((2, nz, piece // 4, LANES), BF),
            vmem((2, piece // 4, LANES), BF),
            vmem((2, piece, LANES), BF),
            dma((7,)), dma((2,)), dma((2,)), dma((2,)), dma((2,)), dma((2,)), dma((2,)), dma((2,)), dma((2,)),
            dma((2,)), dma((2,)), dma((2,)), dma((2,)), dma((2, chips - 1)), dma((2,)), dma((2,)),
        ],
        compiler_params=pltpu.CompilerParams(collective_id=0, has_side_effects=True, vmem_limit_bytes=VMEM_LIMIT),
        name="main",
    )(
        live, tokens.reshape(rows, width), cotangent.reshape(out_slots, 4, out_width), w_qkv, w_out, w_pool,
        gain_one, gain_two,
    )

    scale = 1.0 / math.sqrt(img_dev * nz * out_slots * units)
    out, grad_tokens, grad_qkv, grad_out, grad_pool, one, two = pl.pallas_call(
        functools.partial(unpack_kernel, scale),
        out_shape=(
            sd((out_slots, 4, out_width), BF), sd((rows, width), BF), sd((width, 3 * width), F32),
            sd((width, width), F32), sd((width, out_width), F32), sd((width,), F32), sd((width,), F32),
        ),
        in_specs=whole(3),
        out_specs=whole(7),
        compiler_params=pltpu.CompilerParams(vmem_limit_bytes=VMEM_LIMIT),
        name="unpack",
    )(f, pooled, grad_tok)
    return (
        out.reshape(cotangent.shape), grad_tokens.reshape(tokens.shape), grad_qkv, grad_out, grad_pool, one, two,
    )


def solution(mesh):
    return jax.shard_map(
        local,
        mesh=mesh,
        in_specs=(
            P("img", "unit", None, None), P("img", "unit"), P("img", "unit", None, None),
            P(), P(), P(), P(), P(),
        ),
        out_specs=(P("img", "unit", None, None), P("img", "unit", None, None), P(), P(), P(), P(), P()),
        check_vma=False,
    )
```

time: 80.3 us -> 59.5 us (0.74)
  Pallas kernels: 71.3 us -> 58 us
  local copies, waits for them, and re-layouts: 6.11 us -> 0 us
  other arithmetic: 1.19 us -> 0 us
    pallas_call x4 -> x2, Pallas kernels: 71.3 us -> 58 us  [the longest x1 55.2 us: local(): pl.pallas_call(main_kernel, out_shape=(sd((2 * HALF, LANES), BF), sd((cro...]
    unnamed x12 -> x0, local copies, waits for them, and re-layouts: 4.6 us -> none
    reshape x2 -> x0, local copies, waits for them, and re-layouts: 1.51 us -> none  [the longest x1 0.86 us: local(): cot = cotangent.reshape(crows, out_width)]
    pallas_call x2 -> x0, other arithmetic: 1.19 us -> none  [local(): pl.pallas_call(functools.partial(unpack_kernel, chips, scale), out_shape=...]
where the time goes in v2:
time: 59.5 us; the launch traced here: 59.3 us
  Pallas kernels  58 us (97%)
  between operations  1.29 us (2%)
    pallas_call x1, Pallas kernels, local(): pl.pallas_call(main_kernel, out_shape=(sd((2 * HALF, LANES), BF), sd((cro...  55.2 us
    pallas_call x1, Pallas kernels, local(): pl.pallas_call(functools.partial(unpack_kernel, scale), out_shape=(sd((ou...  2.83 us

profile of v2, /device:TPU:1, one launch (start us, length us, event | category | flops | bytes accessed | tf_op | source)
XLA Modules:
  0.0 59.3 jit_solution(18021743257347219395)
XLA Ops:
  1.3 55.2 %main.1 = (bf16[4096,128]{1,0:T(8,128)(2,1)}, bf16[48,576]{1,0:T(8,128)(2,1)}, bf16[384,288]{1,0:T(8,128)(2,1)}) custom-call(s32[1,1]{1,0:T(1,128)S(6)} %copy.15.live_ref, bf16[384,288]{1,0:T(8,128)(2,1)} %bitcast.4, bf16[12,4,576]{2,1,0:T(4,128)(2,1)} %bitcast.5, bf16[288,864]{1,0:T(8,128)(2,1)} %w_qkv_hbm.1, bf16[288,288]{1,0:T(8,128)(2,1)} %w_out_hbm.1, ...), custom_call_target="tpu_custom_call" | custom-call | tf_op jit(solution)/shard_map/main/pallas_call | solution.py:382
  56.5 2.8 %unpack.1 = (bf16[12,4,576]{2,1,0:T(4,128)(2,1)}, bf16[384,288]{1,0:T(8,128)(2,1)}, f32[288,864]{1,0:T(8,128)}, f32[288,288]{1,0:T(8,128)}, f32[288,576]{1,0:T(8,128)}, /*index=5*/f32[288]{0:T(512)}, f32[288]{0:T(512)}) custom-call(bf16[4096,128]{1,0:T(8,128)(2,1)} %get-tuple-element.17.f_ref, bf16[48,576]{1,0:T(8,128)(2,1)} %get-tuple-element.18.pooled_ref, ...), custom_call_target="tpu_custom_call" | custom-call | tf_op jit(solution)/shard_map/unpack/pallas_call | solution.py:425

commit v3 on v2

--- a/solution.py
+++ b/solution.py
@@ -20,6 +20,7 @@
 HALF = 2048
 AROUND = {1: (0,), 2: (1, 0), 4: (2, 1, 3, 0)}
 VMEM_LIMIT = 62 * 1024 * 1024
+UNPACK_LIMIT = 24 * 1024 * 1024
 
 
 def nn(a, b):
@@ -81,9 +82,9 @@
     f_ref, pooled_out, grad_tokens_ref,
     tok_ref, cot_ref, w_qkv_ref, w_out_ref, w_pool_ref, gain_one_ref, gain_two_ref,
     counts_ref, cots_ref, pooled_ref, prev_ref, g_ref, n_one_ref, n_two_ref, gr_ref, qkv_ref, mixed_ref, gqkv_ref,
-    att_ref, r_one, s_ref, r_two, t_ref, r_three, u_ref, w_ref,
+    att_ref, r_one, s_ref, r_two, t_ref, r_three, u_ref, line_ready,
     in_sems, count_sems, cot_sems, pool_sems, one_send, one_recv, two_send, two_recv, three_send, three_recv,
-    four_send, four_recv, five_send, five_recv, six_send, six_recv,
+    five_send, five_recv, six_send, six_recv,
 ):
     rows, width = tok_ref.shape
     crows = cots_ref.shape[0] // 2
@@ -133,10 +134,15 @@
     get_w_pool = fetch(6, w_pool_hbm, w_pool_ref)
 
     barrier = pltpu.get_barrier_semaphore()
-    for d in range(1, nz):
+    reach = nz // 4
+    near = [d for d in range(1, nz) if min(d, nz - d) <= reach]
+    for d in near:
         pl.semaphore_signal(barrier, inc=1, device_id={"img": lax.rem(z + d, nz)}, device_id_type=MESH)
-    for d in range(1, units):
-        pl.semaphore_signal(barrier, inc=1, device_id={"unit": lax.rem(me + d, units)}, device_id_type=MESH)
+    for dx, dy in plane:
+        for which in range(2):
+            there = chip_at(dx, dy) * 2 + which
+            pl.semaphore_signal(barrier, inc=1, device_id={"unit": there}, device_id_type=MESH)
+    pl.semaphore_signal(barrier, inc=1, device_id={"unit": sibling}, device_id_type=MESH)
 
     def half_of(part, which):
         return pl.ds(pl.multiple_of(part * HALF + which * half, half), half)
@@ -171,34 +177,33 @@
 
     mine = pl.ds(pl.multiple_of(lax.rem(z, 4) * tile, tile), tile)
 
+    def place(part, which_core, which_chip):
+        return pl.ds(pl.multiple_of(part * HALF + which_core * half + which_chip * piece, piece), piece)
+
     def line_add(part):
         drain(r_three.at[part, pl.ds(0, nz - 1)], three_recv.at[part])
         total = r_three[part, 0].astype(F32)
         for k in range(1, nz):
             total = total + r_three[part, k].astype(F32)
         u_ref[part] = total.astype(BF)
-        for d in (2, 1, nz - 1):
-            push(u_ref.at[part], w_ref.at[part, mine], four_send.at[part], four_recv.at[part], img=lax.rem(z + d, nz))
-        w_ref[part, mine, :] = u_ref[part]
-
-    def place(part, which_core, which_chip):
-        return pl.ds(pl.multiple_of(part * HALF + which_core * half + which_chip * piece, piece), piece)
-
-    def plane_spread(part):
-        drain(w_ref.at[part, pl.ds(0, 3 * tile)], four_recv.at[part])
-        here = place(part, core, chip)
-        for k, (dx, dy) in enumerate(plane):
-            push(
-                w_ref.at[part], f_ref.at[here], five_send.at[part], five_recv.at[part, k],
-                unit=chip_at(dx, dy) * 2 + core,
-            )
-        f_ref[here, :] = w_ref[part]
-        push(w_ref.at[part], f_ref.at[here], six_send.at[part], six_recv.at[part], unit=sibling)
+        start = part * HALF + core * half + chip * piece + lax.rem(z, 4) * tile
+        here = pl.ds(pl.multiple_of(start, tile), tile)
+        for k, (dx, dy) in enumerate(plane + [(0, 0)]):
+            for d in (2, 1, nz - 1, 0):
+                if k < chips - 1 or d > 0:
+                    push(
+                        u_ref.at[part], f_ref.at[here], five_send.at[part], five_recv.at[part, k],
+                        img=lax.rem(z + d, nz), unit=chip_at(dx, dy) * 2 + core,
+                    )
+        f_ref[here, :] = u_ref[part]
 
     def pair_spread(part):
-        for k, (dx, dy) in reversed(list(enumerate(plane))):
+        for k, (dx, dy) in reversed(list(enumerate(plane + [(0, 0)]))):
             there = place(part, core, chip_at(nx - dx, ny - dy))
-            drain(f_ref.at[there], five_recv.at[part, k])
+            if k < chips - 1:
+                drain(f_ref.at[there], five_recv.at[part, k])
+            else:
+                drain(f_ref.at[pl.ds(0, 3 * tile)], five_recv.at[part, k])
             push(f_ref.at[there], f_ref.at[there], six_send.at[part], six_recv.at[part], unit=sibling)
 
     get_tok.wait()
@@ -226,9 +231,14 @@
     get_cot.wait()
     cots_ref[:crows, :] = cot_ref[...].reshape(crows, cots_ref.shape[1])
     counts_ref[me] = jnp.full((8, LANES), live_ref[0, 0], jnp.int32)
-    pl.semaphore_wait(barrier, nz + units - 2)
-    for d in range(1, units):
-        push(counts_ref.at[me], counts_ref.at[me], count_sems.at[0], count_sems.at[1], unit=lax.rem(me + d, units))
+    pl.semaphore_wait(barrier, len(near) + units - 1)
+    for d in (reach, nz - reach):
+        pl.semaphore_signal(line_ready, inc=1, device_id={"img": lax.rem(z + d, nz)}, device_id_type=MESH)
+    for dx, dy in plane:
+        for which in range(2):
+            there = chip_at(dx, dy) * 2 + which
+            push(counts_ref.at[me], counts_ref.at[me], count_sems.at[0], count_sems.at[1], unit=there)
+    push(counts_ref.at[me], counts_ref.at[me], count_sems.at[0], count_sems.at[1], unit=sibling)
     cot_copy = push(
         cots_ref.at[pl.ds(0, crows)], cots_ref.at[pl.ds(crows, crows)], cot_sems.at[0], cot_sems.at[1],
         unit=lax.rem(me + units - 1, units),
@@ -254,12 +264,6 @@
     gather = selection((ranked, rows), 1, shift[:, 0:1], live)
     spread = selection((rows, ranked), 0, shift[:, :ranked], live)
     grouped = (nn(gather, high) + nn(gather, low)).astype(BF)
-    pooled_ref[...] = nn(grouped, w_pool_ref[...]).astype(BF)
-    pooled_copy = push(
-        pooled_ref.at[pl.ds(crows, crows)], prev_ref, pool_sems.at[0], pool_sems.at[1],
-        unit=lax.rem(me + 1, units),
-    )
-
     cot_copy.wait_recv()
     cots = cots_ref[...]
     grad_pool = tn(grouped, cots).astype(BF)
@@ -305,18 +309,22 @@
     g_normed = nt(g_qkv, w_qkv_ref[...])
     g_ref[HALF + 2016 : HALF + 2048, :] = gain_rows(jnp.sum(g_normed * n_one, axis=0, keepdims=True))
     pair_send(1)
+    pooled_ref[...] = nn(grouped, w_pool_ref[...]).astype(BF)
+    pooled_copy = push(
+        pooled_ref.at[pl.ds(crows, crows)], prev_ref, pool_sems.at[0], pool_sems.at[1],
+        unit=lax.rem(me + 1, units),
+    )
     g_input = norm_back(g_normed * gain_one_ref[...], n_one, p_one)
     grad_tokens_ref[...] = (gr_ref[...] + g_input).astype(BF)
 
     pair_add(1)
+    pl.semaphore_wait(line_ready, 2)
     plane_add(0)
     pooled_copy.wait_recv()
     pooled_out[...] = pooled_ref[:crows, :] + prev_ref[...]
     plane_add(1)
     line_add(0)
-    plane_spread(0)
     line_add(1)
-    plane_spread(1)
     pair_spread(0)
     pair_spread(1)
 
@@ -324,8 +332,7 @@
         drain(g_ref.at[pl.ds(0, half)], one_send.at[part])
         drain(r_two.at[part], two_send.at[part])
         drain(r_three.at[part, pl.ds(0, nz - 1)], three_send.at[part])
-        drain(w_ref.at[part, pl.ds(0, 3 * tile)], four_send.at[part])
-        drain(f_ref.at[pl.ds(0, half - piece)], five_send.at[part])
+        drain(f_ref.at[pl.ds(0, half - tile)], five_send.at[part])
         drain(f_ref.at[pl.ds(0, half)], six_send.at[part])
         drain(f_ref.at[pl.ds(0, half)], six_recv.at[part])
     drain(others, count_sems.at[0])
@@ -381,7 +388,7 @@
 
     f, pooled, grad_tok = pl.pallas_call(
         main_kernel,
-        out_shape=(sd((2 * HALF, LANES), BF), sd((crows, out_width), BF), sd((rows, width), BF)),
+        out_shape=(vmem((2 * HALF, LANES), BF), vmem((crows, out_width), BF), vmem((rows, width), BF)),
         in_specs=[pl.BlockSpec(memory_space=pltpu.SMEM)] + whole(7, pltpu.HBM),
         out_specs=whole(3),
         scratch_shapes=[
@@ -410,9 +417,9 @@
             vmem((2, piece, LANES), BF),
             vmem((2, nz, piece // 4, LANES), BF),
             vmem((2, piece // 4, LANES), BF),
-            vmem((2, piece, LANES), BF),
+            pltpu.SemaphoreType.REGULAR,
             dma((7,)), dma((2,)), dma((2,)), dma((2,)), dma((2,)), dma((2,)), dma((2,)), dma((2,)), dma((2,)),
-            dma((2,)), dma((2,)), dma((2,)), dma((2,)), dma((2, chips - 1)), dma((2,)), dma((2,)),
+            dma((2,)), dma((2,)), dma((2, chips)), dma((2,)), dma((2,)),
         ],
         compiler_params=pltpu.CompilerParams(collective_id=0, has_side_effects=True, vmem_limit_bytes=VMEM_LIMIT),
         name="main",
@@ -430,7 +437,7 @@
         ),
         in_specs=whole(3),
         out_specs=whole(7),
-        compiler_params=pltpu.CompilerParams(vmem_limit_bytes=VMEM_LIMIT),
+        compiler_params=pltpu.CompilerParams(vmem_limit_bytes=UNPACK_LIMIT),
         name="unpack",
     )(f, pooled, grad_tok)
     return (

time: 59.5 us -> 54.8 us (0.921)
  Pallas kernels: 58 us -> 53.3 us
    pallas_call x1, Pallas kernels: 55.2 us -> 51.8 us  [local(): pl.pallas_call(main_kernel, out_shape=(vmem((2 * HALF, LANES), BF), vmem(...]
    pallas_call x1, Pallas kernels: 2.83 us -> 1.52 us  [local(): pl.pallas_call(functools.partial(unpack_kernel, scale), out_shape=(sd((ou...]
where the time goes in v3:
time: 54.8 us; the launch traced here: 54.6 us
  Pallas kernels  53.3 us (97%)
  between operations  1.29 us (2%)
    pallas_call x1, Pallas kernels, local(): pl.pallas_call(main_kernel, out_shape=(vmem((2 * HALF, LANES), BF), vmem(...  51.8 us
    pallas_call x1, Pallas kernels, local(): pl.pallas_call(functools.partial(unpack_kernel, scale), out_shape=(sd((ou...  1.52 us

profile of v3, /device:TPU:1, one launch (start us, length us, event | category | flops | bytes accessed | tf_op | source)
XLA Modules:
  0.0 54.6 jit_solution(9857049112801985926)
XLA Ops:
  1.3 51.8 %main.1 = (bf16[4096,128]{1,0:T(8,128)(2,1)S(1)}, bf16[48,576]{1,0:T(8,128)(2,1)S(1)}, bf16[384,288]{1,0:T(8,128)(2,1)S(1)}) custom-call(s32[1,1]{1,0:T(1,128)S(6)} %copy.15.live_ref, bf16[384,288]{1,0:T(8,128)(2,1)} %bitcast.4, bf16[12,4,576]{2,1,0:T(4,128)(2,1)} %bitcast.5, bf16[288,864]{1,0:T(8,128)(2,1)} %w_qkv_hbm.1, bf16[288,288]{1,0:T(8,128)(2,1)} %w_out_hbm.1, ...), custom_call_target="tpu_custom_call" | custom-call | tf_op jit(solution)/shard_map/main/pallas_call | solution.py:389
  53.1 1.5 %unpack.1 = (bf16[12,4,576]{2,1,0:T(4,128)(2,1)}, bf16[384,288]{1,0:T(8,128)(2,1)}, f32[288,864]{1,0:T(8,128)}, f32[288,288]{1,0:T(8,128)}, f32[288,576]{1,0:T(8,128)}, /*index=5*/f32[288]{0:T(512)}, f32[288]{0:T(512)}) custom-call(bf16[4096,128]{1,0:T(8,128)(2,1)S(1)} %get-tuple-element.17.f_ref, bf16[48,576]{1,0:T(8,128)(2,1)S(1)} %get-tuple-element.18.pooled_ref, ...), custom_call_target="tpu_custom_call" | custom-call | tf_op jit(solution)/shard_map/unpack/pallas_call | solution.py:432

commit v4 on v3

--- a/solution.py
+++ b/solution.py
@@ -47,13 +47,16 @@
     return inv_scale * (grad_norm - first - normed_v * second)
 
 
-def selection(shape, token_dim, shift, live):
+def slot_map(shape, token_dim, live):
     token = lax.broadcasted_iota(jnp.int32, shape, token_dim)
-    row = lax.broadcasted_iota(jnp.int32, shape, 1 - token_dim)
+    row = lax.broadcasted_iota(jnp.int32, shape, 1 - token_dim) & (LANES - 1)
     slot = token >> 4
     group = ((token >> 3) & 1) * 2 + ((token >> 1) & 1)
-    hit = (row == (shift + slot) * 4 + group) & (slot < live)
-    return jnp.where(hit, 0.25, 0.0).astype(BF)
+    return jnp.where(slot < live, row - slot * 4 - group, -1)
+
+
+def select(mapped, shift):
+    return jnp.where(mapped == shift, 0.25, 0.0).astype(BF)
 
 
 def head_rows(block):
@@ -69,6 +72,16 @@
     return jnp.concatenate([rows[h * BLK : (h + 1) * BLK] for h in range(HEADS)], axis=1)
 
 
+def split(values):
+    high = values.astype(BF)
+    return high, (values - high.astype(F32)).astype(BF)
+
+
+def scores_back(att, g_att, keys):
+    inner = jnp.sum(g_att * att, axis=keys, keepdims=True)
+    return (att * (g_att - inner) * HEAD_DIM ** (-0.5)).astype(BF)
+
+
 def gain_rows(total):
     row = lax.broadcasted_iota(jnp.int32, (32, LANES), 0)
     last = jnp.concatenate([total[:, 256:], jnp.zeros((1, 96), F32)], axis=1)
@@ -81,10 +94,10 @@
     live_ref, tok_hbm, cot_hbm, w_qkv_hbm, w_out_hbm, w_pool_hbm, gain_one_hbm, gain_two_hbm,
     f_ref, pooled_out, grad_tokens_ref,
     tok_ref, cot_ref, w_qkv_ref, w_out_ref, w_pool_ref, gain_one_ref, gain_two_ref,
-    counts_ref, cots_ref, pooled_ref, prev_ref, g_ref, n_one_ref, n_two_ref, gr_ref, qkv_ref, mixed_ref, gqkv_ref,
-    att_ref, r_one, s_ref, r_two, t_ref, r_three, u_ref, line_ready,
+    counts_ref, cots_ref, pooled_ref, prev_ref, g_ref, n_one_ref, n_two_ref, gr_ref, qkv_ref, mixed_ref, gqkv_ref, gmix_ref, to_rows, to_tokens, h_rows,
+    att_ref, att_t, q_rows, k_rows, normed_t, mixed_t, r_one, s_ref, r_two, t_ref, r_three, u_ref, line_ready,
     in_sems, count_sems, cot_sems, pool_sems, one_send, one_recv, two_send, two_recv, three_send, three_recv,
-    five_send, five_recv, six_send, six_recv,
+    five_send, five_recv, six_send, six_recv, line_send,
 ):
     rows, width = tok_ref.shape
     crows = cots_ref.shape[0] // 2
@@ -125,14 +138,6 @@
     def drain(ref, sem):
         pltpu.make_async_copy(ref, ref, sem).wait()
 
-    get_tok = fetch(0, tok_hbm, tok_ref)
-    get_gain_one = fetch(1, gain_one_hbm, gain_one_ref)
-    get_w_qkv = fetch(2, w_qkv_hbm, w_qkv_ref)
-    get_cot = fetch(3, cot_hbm, cot_ref)
-    get_w_out = fetch(4, w_out_hbm, w_out_ref)
-    get_gain_two = fetch(5, gain_two_hbm, gain_two_ref)
-    get_w_pool = fetch(6, w_pool_hbm, w_pool_ref)
-
     barrier = pltpu.get_barrier_semaphore()
     reach = nz // 4
     near = [d for d in range(1, nz) if min(d, nz - d) <= reach]
@@ -144,14 +149,35 @@
             pl.semaphore_signal(barrier, inc=1, device_id={"unit": there}, device_id_type=MESH)
     pl.semaphore_signal(barrier, inc=1, device_id={"unit": sibling}, device_id_type=MESH)
 
+    get_tok = fetch(0, tok_hbm, tok_ref)
+    get_gain_one = fetch(1, gain_one_hbm, gain_one_ref)
+    get_w_qkv = fetch(2, w_qkv_hbm, w_qkv_ref)
+    get_cot = fetch(3, cot_hbm, cot_ref)
+    get_w_out = fetch(4, w_out_hbm, w_out_ref)
+    get_gain_two = fetch(5, gain_two_hbm, gain_two_ref)
+    get_w_pool = fetch(6, w_pool_hbm, w_pool_ref)
+
     def half_of(part, which):
         return pl.ds(pl.multiple_of(part * HALF + which * half, half), half)
 
     def pair_send(part):
-        push(g_ref.at[half_of(part, 1 - core)], r_one.at[part], one_send.at[part], one_recv.at[part], unit=sibling)
+        count = half - 32 * part
+        push(
+            g_ref.at[pl.ds(pl.multiple_of(part * HALF + (1 - core) * half, half), count)],
+            r_one.at[part, pl.ds(0, count)], one_send.at[part], one_recv.at[part], unit=sibling,
+        )
+
+    def pair_send_last():
+        start = HALF + (1 - core) * half + half - 32
+        push(
+            g_ref.at[pl.ds(pl.multiple_of(start, 32), 32)], r_one.at[1, pl.ds(half - 32, 32)],
+            one_send.at[2], one_recv.at[2], unit=sibling,
+        )
 
     def pair_add(part):
-        drain(r_one.at[part], one_recv.at[part])
+        drain(r_one.at[part, pl.ds(0, half - 32 * part)], one_recv.at[part])
+        if part == 1:
+            drain(r_one.at[1, pl.ds(half - 32, 32)], one_recv.at[2])
         own = g_ref[half_of(part, core), :]
         s_ref[part] = (own.astype(F32) + r_one[part].astype(F32)).astype(BF)
         for k, (dx, dy) in enumerate(plane):
@@ -167,7 +193,7 @@
         for k in range(chips - 1):
             total = total + r_two[part, k].astype(F32)
         t_ref[part] = total.astype(BF)
-        for d in range(1, nz):
+        for d in sorted(range(1, nz), key=lambda d: -min(d, nz - d)):
             there = lax.rem(z + d, nz)
             push(
                 t_ref.at[part, pl.ds(pl.multiple_of(lax.rem(there, 4) * tile, tile), tile)], r_three.at[part, z],
@@ -188,6 +214,14 @@
         u_ref[part] = total.astype(BF)
         start = part * HALF + core * half + chip * piece + lax.rem(z, 4) * tile
         here = pl.ds(pl.multiple_of(start, tile), tile)
+        if part == 0:
+            for d in (2, 1, nz - 1):
+                push(
+                    u_ref.at[part], f_ref.at[here], line_send, five_recv.at[part, chips - 1],
+                    img=lax.rem(z + d, nz),
+                )
+            f_ref[here, :] = u_ref[part]
+            return
         for k, (dx, dy) in enumerate(plane + [(0, 0)]):
             for d in (2, 1, nz - 1, 0):
                 if k < chips - 1 or d > 0:
@@ -197,12 +231,18 @@
                     )
         f_ref[here, :] = u_ref[part]
 
+    def plane_spread(part):
+        drain(f_ref.at[pl.ds(0, 3 * tile)], five_recv.at[part, chips - 1])
+        own = f_ref.at[place(part, core, chip)]
+        for k, (dx, dy) in enumerate(plane):
+            push(own, own, five_send.at[part], five_recv.at[part, k], unit=chip_at(dx, dy) * 2 + core)
+
     def pair_spread(part):
         for k, (dx, dy) in reversed(list(enumerate(plane + [(0, 0)]))):
             there = place(part, core, chip_at(nx - dx, ny - dy))
             if k < chips - 1:
                 drain(f_ref.at[there], five_recv.at[part, k])
-            else:
+            elif part == 1:
                 drain(f_ref.at[pl.ds(0, 3 * tile)], five_recv.at[part, k])
             push(f_ref.at[there], f_ref.at[there], six_send.at[part], six_recv.at[part], unit=sibling)
 
@@ -214,23 +254,9 @@
     get_w_qkv.wait()
     qkv_ref[...] = nn(normed, w_qkv_ref[...]).astype(BF)
 
-    same = (
-        lax.broadcasted_iota(jnp.int32, (HEADS * BLK, BLK), 0) & (BLK - 1)
-    ) >> 4 == lax.broadcasted_iota(jnp.int32, (HEADS * BLK, BLK), 1) >> 4
-    for b in range(blocks):
-        span = slice(b * BLK, (b + 1) * BLK)
-        query = head_rows(qkv_ref[span, :width])
-        scores = nt(query, qkv_ref[span, width : 2 * width]) * factor
-        scores = jnp.where(same, scores, -1e30)
-        e = jnp.exp(scores - jnp.max(scores, axis=-1, keepdims=True))
-        att = e * (1.0 / jnp.sum(e, axis=-1, keepdims=True))
-        att_ref[b] = att
-        value = head_rows(qkv_ref[span, 2 * width :])
-        mixed_ref[span, :] = nn(heads_to_lanes(att.astype(BF)), value).astype(BF)
-
     get_cot.wait()
     cots_ref[:crows, :] = cot_ref[...].reshape(crows, cots_ref.shape[1])
-    counts_ref[me] = jnp.full((8, LANES), live_ref[0, 0], jnp.int32)
+    counts_ref[me] = jnp.full((1, LANES), live_ref[0, 0], jnp.int32)
     pl.semaphore_wait(barrier, len(near) + units - 1)
     for d in (reach, nz - reach):
         pl.semaphore_signal(line_ready, inc=1, device_id={"img": lax.rem(z + d, nz)}, device_id_type=MESH)
@@ -244,36 +270,60 @@
         unit=lax.rem(me + units - 1, units),
     )
 
+    same = (
+        lax.broadcasted_iota(jnp.int32, (HEADS * BLK, BLK), 0) & (BLK - 1)
+    ) >> 4 == lax.broadcasted_iota(jnp.int32, (HEADS * BLK, BLK), 1) >> 4
+    for b in range(blocks):
+        span = slice(b * BLK, (b + 1) * BLK)
+        q_rows[b] = head_rows(qkv_ref[span, :width])
+        k_rows[b] = head_rows(qkv_ref[span, width : 2 * width])
+        scores = nt(q_rows[b], qkv_ref[span, width : 2 * width]) * factor
+        scores = jnp.where(same, scores, -1e30)
+        e = jnp.exp(scores - jnp.max(scores, axis=-1, keepdims=True))
+        att = e * (1.0 / jnp.sum(e, axis=-1, keepdims=True))
+        att_ref[b] = att
+        att_t[b] = att.astype(BF).T
+        value = head_rows(qkv_ref[span, 2 * width :])
+        mixed_ref[span, :] = nn(heads_to_lanes(att.astype(BF)), value).astype(BF)
+    normed_t[...] = normed.T
+
     get_w_out.wait()
     get_gain_two.wait()
     n_two, p_two = normalize(tok_ref[...].astype(F32) + nn(mixed_ref[...], w_out_ref[...]))
     n_two_ref[...] = n_two
-    y = n_two * gain_two_ref[...]
-    high = y.astype(BF)
-    low = (y - high.astype(F32)).astype(BF)
-
+    high, low = split(n_two)
+    mixed_t[...] = mixed_ref[...].T
+    live = live_ref[0, 0]
+    to_rows[...] = slot_map(to_rows.shape, 1, live)
+    to_tokens[...] = slot_map(to_tokens.shape, 0, live)
     get_w_pool.wait()
+    cot_copy.wait_recv()
+    cots = cots_ref[...]
+    g_grouped = nt(cots, w_pool_ref[...])
+    h_grouped = g_grouped * gain_two_ref[...]
+    h_high, h_low = split(h_grouped - jnp.mean(h_grouped, axis=-1, keepdims=True))
+    gap = jnp.zeros((LANES - h_high.shape[0], width), BF)
+    h_rows[...] = jnp.concatenate([h_high, gap, h_low, gap], axis=0)
+
     others = counts_ref.at[pl.ds(0, units - 1)]
     drain(others, count_sems.at[1])
-    before = jnp.zeros((8, LANES), jnp.int32)
+    before = jnp.zeros((1, LANES), jnp.int32)
     for k in range(units):
         before = before + jnp.where(k < me, counts_ref[k], 0)
-    shift = before[0:1, :] - me * out_slots
-    live = live_ref[0, 0]
-    ranked = 2 * crows
-    gather = selection((ranked, rows), 1, shift[:, 0:1], live)
-    spread = selection((rows, ranked), 0, shift[:, :ranked], live)
-    grouped = (nn(gather, high) + nn(gather, low)).astype(BF)
-    cot_copy.wait_recv()
-    cots = cots_ref[...]
-    grad_pool = tn(grouped, cots).astype(BF)
-    g_scaled = nt(nn(spread, cots).astype(BF), w_pool_ref[...])
+    shift = (before[:, 0:1] - me * out_slots) * 4
+
+    h = nn(select(to_tokens[...], shift), h_rows[...])
     n_two = n_two_ref[...]
-    g_ref[2016:2048, :] = gain_rows(jnp.sum(g_scaled * n_two, axis=0, keepdims=True))
-    g_resid = norm_back(g_scaled * gain_two_ref[...], n_two, p_two)
+    g_resid = p_two * (h - n_two * jnp.mean(h * n_two, axis=-1, keepdims=True))
     gr_ref[...] = g_resid
     resid_b = g_resid.astype(BF)
-    grad_out = tn(mixed_ref[...], resid_b).astype(BF)
+
+    gather = select(to_rows[...], shift)
+    mean_two = nn(gather, high) + nn(gather, low)
+    grouped = (mean_two * gain_two_ref[...]).astype(BF)
+    g_ref[2016:2048, :] = gain_rows(jnp.sum(g_grouped * mean_two, axis=0, keepdims=True))
+    grad_pool = tn(grouped, cots).astype(BF)
+    grad_out = nn(mixed_t[...], resid_b).astype(BF)
     for k in range(4):
         g_ref[width * k : width * (k + 1), :] = grad_pool[:, LANES * k : LANES * (k + 1)]
     g_ref[width * 4 : width * 5, :] = jnp.concatenate(
@@ -283,32 +333,39 @@
     g_ref[width * 6 : width * 7, :] = grad_out[:, 128:256]
     pair_send(0)
 
-    mixed_ref[...] = nt(resid_b, w_out_ref[...]).astype(BF)
+    gmix_ref[...] = nt(resid_b, w_out_ref[...]).astype(BF)
+
+    def scores_of(b):
+        span = slice(b * BLK, (b + 1) * BLK)
+        rows_b = head_rows(gmix_ref[span, :])
+        return rows_b, nt(rows_b, qkv_ref[span, 2 * width :])
+
+    ahead = scores_of(0)
     for b in range(blocks):
         span = slice(b * BLK, (b + 1) * BLK)
-        att = att_ref[b]
-        g_mixed = head_rows(mixed_ref[span, :])
-        g_att = nt(g_mixed, qkv_ref[span, 2 * width :])
-        g_value = tn(att.astype(BF), g_mixed).astype(BF)
-        g_scores = (att * (g_att - jnp.sum(g_att * att, axis=-1, keepdims=True)) * factor).astype(BF)
-        g_query = nn(heads_to_lanes(g_scores), head_rows(qkv_ref[span, width : 2 * width])).astype(BF)
-        g_key = tn(g_scores, head_rows(qkv_ref[span, :width])).astype(BF)
+        g_mixed, g_att = ahead
+        if b + 1 < blocks:
+            ahead = scores_of(b + 1)
+        g_value = nn(att_t[b], g_mixed).astype(BF)
+        g_scores = scores_back(att_ref[b], g_att, -1)
+        g_query = nn(heads_to_lanes(g_scores), k_rows[b]).astype(BF)
+        g_key = tn(g_scores, q_rows[b]).astype(BF)
         gqkv_ref[span, :] = jnp.concatenate([g_query, g_key, g_value], axis=1)
         if b == blocks - 2:
             pair_add(0)
 
     g_qkv = gqkv_ref[...]
     n_one = n_one_ref[...]
-    normed = (n_one * gain_one_ref[...]).astype(BF)
-    grad_qkv = tn(normed, g_qkv).astype(BF)
+    grad_qkv = nn(normed_t[...], g_qkv).astype(BF)
     for k in range(6):
         g_ref[HALF + width * k : HALF + width * (k + 1), :] = grad_qkv[:, LANES * k : LANES * (k + 1)]
     g_ref[HALF + width * 6 : HALF + width * 7, :] = jnp.concatenate(
         [grad_qkv[:, 768:864], jnp.zeros((width, 32), BF)], axis=1
     )
+    pair_send(1)
     g_normed = nt(g_qkv, w_qkv_ref[...])
     g_ref[HALF + 2016 : HALF + 2048, :] = gain_rows(jnp.sum(g_normed * n_one, axis=0, keepdims=True))
-    pair_send(1)
+    pair_send_last()
     pooled_ref[...] = nn(grouped, w_pool_ref[...]).astype(BF)
     pooled_copy = push(
         pooled_ref.at[pl.ds(crows, crows)], prev_ref, pool_sems.at[0], pool_sems.at[1],
@@ -324,49 +381,66 @@
     pooled_out[...] = pooled_ref[:crows, :] + prev_ref[...]
     plane_add(1)
     line_add(0)
+    plane_spread(0)
     line_add(1)
     pair_spread(0)
     pair_spread(1)
 
     for part in range(2):
-        drain(g_ref.at[pl.ds(0, half)], one_send.at[part])
+        drain(g_ref.at[pl.ds(0, half - 32 * part)], one_send.at[part])
         drain(r_two.at[part], two_send.at[part])
         drain(r_three.at[part, pl.ds(0, nz - 1)], three_send.at[part])
-        drain(f_ref.at[pl.ds(0, half - tile)], five_send.at[part])
+        drain(f_ref.at[pl.ds(0, half - (piece, tile)[part])], five_send.at[part])
         drain(f_ref.at[pl.ds(0, half)], six_send.at[part])
         drain(f_ref.at[pl.ds(0, half)], six_recv.at[part])
+    drain(g_ref.at[pl.ds(0, 32)], one_send.at[2])
+    drain(f_ref.at[pl.ds(0, 3 * tile)], line_send)
     drain(others, count_sems.at[0])
     cot_copy.wait_send()
     pooled_copy.wait_send()
 
 
 def unpack_kernel(
-    scale, f_ref, pooled_ref, tok_ref, out_ref, grad_tokens_ref, qkv_ref, go_ref, pool_ref, one_ref, two_ref
+    scale, f_ref, pooled_ref, tok_ref, out_hbm, grad_tokens_hbm, qkv_hbm, go_hbm, pool_hbm, one_hbm, two_hbm,
+    out_ref, qkv_ref, go_ref, pool_ref, one_ref, two_ref, sems,
 ):
     width = go_ref.shape[0]
-
-    def rows(start, count):
-        return f_ref[start : start + count, :].astype(F32) * scale
-
-    for k in range(7):
-        early = rows(width * k, width)
-        late = rows(HALF + width * k, width)
-        if k < 6:
-            qkv_ref[:, LANES * k : LANES * (k + 1)] = late
-        else:
-            qkv_ref[:, 768:864] = late[:, :96]
-        if k < 4:
-            pool_ref[:, LANES * k : LANES * (k + 1)] = early
-        elif k == 4:
-            pool_ref[:, 512:576] = early[:, :64]
-            go_ref[:, 256:288] = early[:, 64:96]
-        else:
-            go_ref[:, LANES * (k - 5) : LANES * (k - 4)] = early
-    for start, ref in ((2016, two_ref), (HALF + 2016, one_ref)):
-        last = rows(start, 32)
+    copies = []
+
+    def store(source, target):
+        copy = pltpu.make_async_copy(source, target, sems.at[len(copies)])
+        copy.start()
+        copies.append(copy)
+
+    store(tok_ref, grad_tokens_hbm)
+    step = width // 3
+    for r in range(0, width, step):
+        span = slice(r, r + step)
+
+        def rows(start):
+            return f_ref[start + r : start + r + step, :].astype(F32) * scale
+
+        for k in range(6):
+            qkv_ref[span, LANES * k : LANES * (k + 1)] = rows(HALF + width * k)
+        qkv_ref[span, 768:864] = rows(HALF + width * 6)[:, :96]
+        store(qkv_ref.at[pl.ds(r, step)], qkv_hbm.at[pl.ds(r, step)])
+        for k in range(4):
+            pool_ref[span, LANES * k : LANES * (k + 1)] = rows(width * k)
+        both = rows(width * 4)
+        pool_ref[span, 512:576] = both[:, :64]
+        store(pool_ref.at[pl.ds(r, step)], pool_hbm.at[pl.ds(r, step)])
+        go_ref[span, 256:288] = both[:, 64:96]
+        for k in range(2):
+            go_ref[span, LANES * k : LANES * (k + 1)] = rows(width * (k + 5))
+        store(go_ref.at[pl.ds(r, step)], go_hbm.at[pl.ds(r, step)])
+    for start, ref, target in ((2016, two_ref, two_hbm), (HALF + 2016, one_ref, one_hbm)):
+        last = f_ref[start : start + 32, :].astype(F32) * scale
         ref[...] = jnp.concatenate([last[0:1], last[1:2], last[2:3, :32]], axis=1).reshape(ref.shape)
+        store(ref, target)
     out_ref[...] = pooled_ref[...].reshape(out_ref.shape)
-    grad_tokens_ref[...] = tok_ref[...]
+    store(out_ref, out_hbm)
+    for copy in copies:
+        copy.wait()
 
 
 def whole(count, space=pltpu.VMEM):
@@ -399,7 +473,7 @@
             vmem(w_pool.shape, BF),
             vmem(gain_one.shape, F32),
             vmem(gain_two.shape, F32),
-            vmem((units, 8, LANES), jnp.int32),
+            vmem((units, 1, LANES), jnp.int32),
             vmem((2 * crows, out_width), BF),
             vmem((2 * crows, out_width), BF),
             vmem((crows, out_width), BF),
@@ -410,7 +484,16 @@
             vmem((rows, 3 * width), BF),
             vmem((rows, width), BF),
             vmem((rows, 3 * width), BF),
+            vmem((rows, width), BF),
+            vmem((2 * crows, rows), jnp.int32),
+            vmem((rows, 2 * LANES), jnp.int32),
+            vmem((2 * LANES, width), BF),
             vmem((rows // BLK, HEADS * BLK, BLK), F32),
+            vmem((rows // BLK, BLK, HEADS * BLK), BF),
+            vmem((rows // BLK, HEADS * BLK, width), BF),
+            vmem((rows // BLK, HEADS * BLK, width), BF),
+            vmem((width, rows), BF),
+            vmem((width, rows), BF),
             vmem((2, HALF // 2, LANES), BF),
             vmem((2, HALF // 2, LANES), BF),
             vmem((2, chips - 1, piece, LANES), BF),
@@ -418,8 +501,8 @@
             vmem((2, nz, piece // 4, LANES), BF),
             vmem((2, piece // 4, LANES), BF),
             pltpu.SemaphoreType.REGULAR,
-            dma((7,)), dma((2,)), dma((2,)), dma((2,)), dma((2,)), dma((2,)), dma((2,)), dma((2,)), dma((2,)),
-            dma((2,)), dma((2,)), dma((2, chips)), dma((2,)), dma((2,)),
+            dma((7,)), dma((2,)), dma((2,)), dma((2,)), dma((3,)), dma((3,)), dma((2,)), dma((2,)), dma((2,)),
+            dma((2,)), dma((2,)), dma((2, chips)), dma((2,)), dma((2,)), dma,
         ],
         compiler_params=pltpu.CompilerParams(collective_id=0, has_side_effects=True, vmem_limit_bytes=VMEM_LIMIT),
         name="main",
@@ -436,7 +519,11 @@
             sd((width, width), F32), sd((width, out_width), F32), sd((width,), F32), sd((width,), F32),
         ),
         in_specs=whole(3),
-        out_specs=whole(7),
+        out_specs=whole(7, pl.ANY),
+        scratch_shapes=[
+            vmem((out_slots, 4, out_width), BF), vmem((width, 3 * width), F32), vmem((width, width), F32),
+            vmem((width, out_width), F32), vmem((width,), F32), vmem((width,), F32), dma((13,)),
+        ],
         compiler_params=pltpu.CompilerParams(vmem_limit_bytes=UNPACK_LIMIT),
         name="unpack",
     )(f, pooled, grad_tok)

time: 54.8 us -> 52.3 us (0.954)
  Pallas kernels: 53.3 us -> 50.8 us
    pallas_call x1, Pallas kernels: 51.8 us -> 49.3 us  [local(): pl.pallas_call(main_kernel, out_shape=(vmem((2 * HALF, LANES), BF), vmem(...]
where the time goes in v4:
time: 52.3 us; the launch traced here: 52.1 us
  Pallas kernels  50.8 us (97%)
  between operations  1.29 us (2%)
    pallas_call x1, Pallas kernels, local(): pl.pallas_call(main_kernel, out_shape=(vmem((2 * HALF, LANES), BF), vmem(...  49.3 us
    pallas_call x1, Pallas kernels, local(): pl.pallas_call(functools.partial(unpack_kernel, scale), out_shape=(sd((ou...  1.57 us

profile of v4, /device:TPU:1, one launch (start us, length us, event | category | flops | bytes accessed | tf_op | source)
XLA Modules:
  0.0 52.1 jit_solution(4870769480493949053)
XLA Ops:
  1.3 49.3 %main.1 = (bf16[4096,128]{1,0:T(8,128)(2,1)S(1)}, bf16[48,576]{1,0:T(8,128)(2,1)S(1)}, bf16[384,288]{1,0:T(8,128)(2,1)S(1)}) custom-call(s32[1,1]{1,0:T(1,128)S(6)} %copy.15.live_ref, bf16[384,288]{1,0:T(8,128)(2,1)} %bitcast.4, bf16[12,4,576]{2,1,0:T(4,128)(2,1)} %bitcast.5, bf16[288,864]{1,0:T(8,128)(2,1)} %w_qkv_hbm.1, bf16[288,288]{1,0:T(8,128)(2,1)} %w_out_hbm.1, ...), custom_call_target="tpu_custom_call" | custom-call | tf_op jit(solution)/shard_map/main/pallas_call | solution.py:463
  50.5 1.6 %unpack.1 = (bf16[12,4,576]{2,1,0:T(4,128)(2,1)}, bf16[384,288]{1,0:T(8,128)(2,1)}, f32[288,864]{1,0:T(8,128)}, f32[288,288]{1,0:T(8,128)}, f32[288,576]{1,0:T(8,128)}, /*index=5*/f32[288]{0:T(512)}, f32[288]{0:T(512)}) custom-call(bf16[4096,128]{1,0:T(8,128)(2,1)S(1)} %get-tuple-element.17.f_ref, bf16[48,576]{1,0:T(8,128)(2,1)S(1)} %get-tuple-element.18.pooled_ref, ...), custom_call_target="tpu_custom_call" | custom-call | tf_op jit(solution)/shard_map/unpack/pallas_call | solution.py:515

commit v5 on v4

--- a/solution.py
+++ b/solution.py
@@ -120,7 +120,10 @@
     sibling = me + 1 - 2 * core
     plane = [(dx, dy) for dx in AROUND[nx] for dy in AROUND[ny]][:-1]
 
+    swap = core if nx == ny else 0
+
     def chip_at(dx, dy):
+        dx, dy = dx + swap * (dy - dx), dy + swap * (dx - dy)
         return lax.rem(chip_y + dy, ny) * nx + lax.rem(chip_x + dx, nx)
 
     def fetch(k, source, target):
@@ -351,7 +354,7 @@
         g_query = nn(heads_to_lanes(g_scores), k_rows[b]).astype(BF)
         g_key = tn(g_scores, q_rows[b]).astype(BF)
         gqkv_ref[span, :] = jnp.concatenate([g_query, g_key, g_value], axis=1)
-        if b == blocks - 2:
+        if b == 0:
             pair_add(0)
 
     g_qkv = gqkv_ref[...]
@@ -377,12 +380,12 @@
     pair_add(1)
     pl.semaphore_wait(line_ready, 2)
     plane_add(0)
-    pooled_copy.wait_recv()
-    pooled_out[...] = pooled_ref[:crows, :] + prev_ref[...]
     plane_add(1)
     line_add(0)
     plane_spread(0)
     line_add(1)
+    pooled_copy.wait_recv()
+    pooled_out[...] = pooled_ref[:crows, :] + prev_ref[...]
     pair_spread(0)
     pair_spread(1)
 

time: 52.3 us -> 52 us (level)
  no operation moved by 1% of the time
where the time goes in v5:
time: 52 us; the launch traced here: 51.9 us
  Pallas kernels  50.6 us (97%)
  between operations  1.29 us (2%)
    pallas_call x1, Pallas kernels, local(): pl.pallas_call(main_kernel, out_shape=(vmem((2 * HALF, LANES), BF), vmem(...  49 us
    pallas_call x1, Pallas kernels, local(): pl.pallas_call(functools.partial(unpack_kernel, scale), out_shape=(sd((ou...  1.57 us

profile of v5, /device:TPU:1, one launch (start us, length us, event | category | flops | bytes accessed | tf_op | source)
XLA Modules:
  0.0 51.9 jit_solution(1842083058026141836)
XLA Ops:
  1.3 49.0 %main.1 = (bf16[4096,128]{1,0:T(8,128)(2,1)S(1)}, bf16[48,576]{1,0:T(8,128)(2,1)S(1)}, bf16[384,288]{1,0:T(8,128)(2,1)S(1)}) custom-call(s32[1,1]{1,0:T(1,128)S(6)} %copy.15.live_ref, bf16[384,288]{1,0:T(8,128)(2,1)} %bitcast.4, bf16[12,4,576]{2,1,0:T(4,128)(2,1)} %bitcast.5, bf16[288,864]{1,0:T(8,128)(2,1)} %w_qkv_hbm.1, bf16[288,288]{1,0:T(8,128)(2,1)} %w_out_hbm.1, ...), custom_call_target="tpu_custom_call" | custom-call | tf_op jit(solution)/shard_map/main/pallas_call | solution.py:466
  50.3 1.6 %unpack.1 = (bf16[12,4,576]{2,1,0:T(4,128)(2,1)}, bf16[384,288]{1,0:T(8,128)(2,1)}, f32[288,864]{1,0:T(8,128)}, f32[288,288]{1,0:T(8,128)}, f32[288,576]{1,0:T(8,128)}, /*index=5*/f32[288]{0:T(512)}, f32[288]{0:T(512)}) custom-call(bf16[4096,128]{1,0:T(8,128)(2,1)S(1)} %get-tuple-element.17.f_ref, bf16[48,576]{1,0:T(8,128)(2,1)S(1)} %get-tuple-element.18.pooled_ref, ...), custom_call_target="tpu_custom_call" | custom-call | tf_op jit(solution)/shard_map/unpack/pallas_call | solution.py:518

commit v6 on v5

--- a/solution.py
+++ b/solution.py
@@ -257,22 +257,6 @@
     get_w_qkv.wait()
     qkv_ref[...] = nn(normed, w_qkv_ref[...]).astype(BF)
 
-    get_cot.wait()
-    cots_ref[:crows, :] = cot_ref[...].reshape(crows, cots_ref.shape[1])
-    counts_ref[me] = jnp.full((1, LANES), live_ref[0, 0], jnp.int32)
-    pl.semaphore_wait(barrier, len(near) + units - 1)
-    for d in (reach, nz - reach):
-        pl.semaphore_signal(line_ready, inc=1, device_id={"img": lax.rem(z + d, nz)}, device_id_type=MESH)
-    for dx, dy in plane:
-        for which in range(2):
-            there = chip_at(dx, dy) * 2 + which
-            push(counts_ref.at[me], counts_ref.at[me], count_sems.at[0], count_sems.at[1], unit=there)
-    push(counts_ref.at[me], counts_ref.at[me], count_sems.at[0], count_sems.at[1], unit=sibling)
-    cot_copy = push(
-        cots_ref.at[pl.ds(0, crows)], cots_ref.at[pl.ds(crows, crows)], cot_sems.at[0], cot_sems.at[1],
-        unit=lax.rem(me + units - 1, units),
-    )
-
     same = (
         lax.broadcasted_iota(jnp.int32, (HEADS * BLK, BLK), 0) & (BLK - 1)
     ) >> 4 == lax.broadcasted_iota(jnp.int32, (HEADS * BLK, BLK), 1) >> 4
@@ -288,6 +272,22 @@
         att_t[b] = att.astype(BF).T
         value = head_rows(qkv_ref[span, 2 * width :])
         mixed_ref[span, :] = nn(heads_to_lanes(att.astype(BF)), value).astype(BF)
+        if b == 1:
+            get_cot.wait()
+            cots_ref[:crows, :] = cot_ref[...].reshape(crows, cots_ref.shape[1])
+            counts_ref[me] = jnp.full((1, LANES), live_ref[0, 0], jnp.int32)
+            pl.semaphore_wait(barrier, len(near) + units - 1)
+            for d in (reach, nz - reach):
+                pl.semaphore_signal(line_ready, inc=1, device_id={"img": lax.rem(z + d, nz)}, device_id_type=MESH)
+            cot_copy = push(
+                cots_ref.at[pl.ds(0, crows)], cots_ref.at[pl.ds(crows, crows)], cot_sems.at[0], cot_sems.at[1],
+                unit=lax.rem(me + units - 1, units),
+            )
+            for dx, dy in plane:
+                for which in range(2):
+                    there = chip_at(dx, dy) * 2 + which
+                    push(counts_ref.at[me], counts_ref.at[me], count_sems.at[0], count_sems.at[1], unit=there)
+            push(counts_ref.at[me], counts_ref.at[me], count_sems.at[0], count_sems.at[1], unit=sibling)
     normed_t[...] = normed.T
 
     get_w_out.wait()
@@ -369,6 +369,7 @@
     g_normed = nt(g_qkv, w_qkv_ref[...])
     g_ref[HALF + 2016 : HALF + 2048, :] = gain_rows(jnp.sum(g_normed * n_one, axis=0, keepdims=True))
     pair_send_last()
+    pair_add(1)
     pooled_ref[...] = nn(grouped, w_pool_ref[...]).astype(BF)
     pooled_copy = push(
         pooled_ref.at[pl.ds(crows, crows)], prev_ref, pool_sems.at[0], pool_sems.at[1],
@@ -377,7 +378,6 @@
     g_input = norm_back(g_normed * gain_one_ref[...], n_one, p_one)
     grad_tokens_ref[...] = (gr_ref[...] + g_input).astype(BF)
 
-    pair_add(1)
     pl.semaphore_wait(line_ready, 2)
     plane_add(0)
     plane_add(1)

time: 52 us -> 51.8 us (level)
  no operation moved by 1% of the time
where the time goes in v6:
time: 51.8 us; the launch traced here: 51.7 us
  Pallas kernels  50.4 us (97%)
  between operations  1.29 us (2%)
    pallas_call x1, Pallas kernels, local(): pl.pallas_call(main_kernel, out_shape=(vmem((2 * HALF, LANES), BF), vmem(...  48.8 us
    pallas_call x1, Pallas kernels, local(): pl.pallas_call(functools.partial(unpack_kernel, scale), out_shape=(sd((ou...  1.57 us

profile of v6, /device:TPU:1, one launch (start us, length us, event | category | flops | bytes accessed | tf_op | source)
XLA Modules:
  0.0 51.7 jit_solution(17075276374601917300)
XLA Ops:
  1.3 48.8 %main.1 = (bf16[4096,128]{1,0:T(8,128)(2,1)S(1)}, bf16[48,576]{1,0:T(8,128)(2,1)S(1)}, bf16[384,288]{1,0:T(8,128)(2,1)S(1)}) custom-call(s32[1,1]{1,0:T(1,128)S(6)} %copy.15.live_ref, bf16[384,288]{1,0:T(8,128)(2,1)} %bitcast.4, bf16[12,4,576]{2,1,0:T(4,128)(2,1)} %bitcast.5, bf16[288,864]{1,0:T(8,128)(2,1)} %w_qkv_hbm.1, bf16[288,288]{1,0:T(8,128)(2,1)} %w_out_hbm.1, ...), custom_call_target="tpu_custom_call" | custom-call | tf_op jit(solution)/shard_map/main/pallas_call | solution.py:466
  50.1 1.6 %unpack.1 = (bf16[12,4,576]{2,1,0:T(4,128)(2,1)}, bf16[384,288]{1,0:T(8,128)(2,1)}, f32[288,864]{1,0:T(8,128)}, f32[288,288]{1,0:T(8,128)}, f32[288,576]{1,0:T(8,128)}, /*index=5*/f32[288]{0:T(512)}, f32[288]{0:T(512)}) custom-call(bf16[4096,128]{1,0:T(8,128)(2,1)S(1)} %get-tuple-element.17.f_ref, bf16[48,576]{1,0:T(8,128)(2,1)S(1)} %get-tuple-element.18.pooled_ref, ...), custom_call_target="tpu_custom_call" | custom-call | tf_op jit(solution)/shard_map/unpack/pallas_call | solution.py:518
